TPU v7x, 128 devices: a whole 4x4x4 slice. The times are simulated.
128 devices in a mesh: group: 4 (over x), sub: 32 (over y, z, core).
Axes of the slice: x: 4, y: 4, z: 4, core: 2. Of those that a mesh axis runs over, the one named last changes fastest.
Arguments:
- a_vals: bfloat16 [4096, 9, 128, 128], P(('group', 'sub')), may hold values from -0.5 to 0.5
- a_cols: int32 [4096, 9], P(('group', 'sub')), may hold values from 0 to 47
- p_vals: bfloat16 [4096, 2, 128, 128], P(('group', 'sub')), may hold values from -0.5 to 0.5
- halo_send: int32 [2048], P(('group', 'sub')), may hold values from 0 to 31
- send_slot: int32 [4096, 2, 9, 2], P(('group', 'sub')), may hold values from 0 to 127, as said below
- recv_block: int32 [16384], P(('group', 'sub')), may hold values from 0 to 32
Outputs:
- coarse: float32 [4096, 128, 128], P(('group', 'sub'))
Inputs may be any that keep to these rules, and one draw needn't show every extreme that they name: `a_cols`: values below 32 name the device's own rows, the next 8 the rows received from the previous subdomain, the last 8 those from the next subdomain. `halo_send`: local rows of the sending device; its first 8 entries are for the previous subdomain, the others for the next. `send_slot`: a device number g * 32 + t of any group g, whose sub index t differs from the sending device's sub index by at most 2. `recv_block`: the value 32 means that the sender's partial block is not used.
All inputs are finite; a program needn't handle non-finite values.
Results may differ from a plain program's by a relative error of at most 0.0029.
Values may be sent and summed in bfloat16 or wider, within the bound.
A program may use at most 128 MiB of HBM per device.

v0:
```python
import jax
import jax.numpy as jnp
from jax import lax
from jax.sharding import PartitionSpec as P

OWN = 32


def with_halo(array, sides, width):
    for axis, dim in sides:
        count, length = (lax.axis_size(axis), array.shape[dim])
        up = [(i, (i + 1) % count) for i in range(count - 1)]
        down = [(j, i) for i, j in up]
        last = lax.slice_in_dim(array, length - width, length, axis=dim)
        initial = lax.slice_in_dim(array, 0, width, axis=dim)
        before = lax.ppermute(last, axis, up)
        after = lax.ppermute(initial, axis, down)
        array = jnp.concatenate([before, array, after], axis=dim)
    return array


def select_bf(labels, table):
    count = table.shape[0]
    picker = (labels[:, None] == jnp.arange(count, dtype=jnp.int32)[None, :]).astype(jnp.bfloat16)
    picked = jnp.dot(picker, table.reshape(count, -1), preferred_element_type=jnp.float32)
    return picked.astype(jnp.bfloat16).reshape((labels.shape[0],) + table.shape[1:])


def gather_sum(labels, values, count):
    picker = (jnp.arange(count, dtype=jnp.int32)[:, None] == labels[None, :]).astype(jnp.float32)
    summed = jnp.dot(
        picker,
        values.reshape(values.shape[0], -1),
        precision=lax.Precision.HIGHEST,
        preferred_element_type=jnp.float32,
    )
    return summed.reshape((count,) + values.shape[1:])


def per_device(a_vals, a_cols, p_vals, halo_send, send_slot, recv_block):
    row_count = a_vals.shape[0]
    op_slots = a_vals.shape[1]
    p_slots = p_vals.shape[1]
    block_width = a_vals.shape[-1]
    halo_rows = halo_send.shape[0] // 2
    group_count = lax.axis_size("group")
    sub_count = lax.axis_size("sub")
    devices = group_count * sub_count
    my_sub = lax.axis_index("sub")
    packed = select_bf(halo_send, p_vals)
    framed = with_halo(packed, (("sub", 0),), halo_rows)
    extended = jnp.concatenate(
        [p_vals, framed[:halo_rows], framed[framed.shape[0] - halo_rows :]], axis=0
    )
    block_rows = min(8, row_count)
    block_count = row_count // block_rows

    def advance(window_sums, turn_index):
        first_row = turn_index * block_rows
        op_block = lax.dynamic_slice_in_dim(a_vals, first_row, block_rows, 0)
        col_block = lax.dynamic_slice_in_dim(a_cols, first_row, block_rows, 0)
        own_block = lax.dynamic_slice_in_dim(p_vals, first_row, block_rows, 0)
        slot_block = lax.dynamic_slice_in_dim(send_slot, first_row, block_rows, 0)
        far_rows = select_bf(col_block.reshape(-1), extended)
        far_rows = far_rows.reshape(block_rows, op_slots, p_slots, block_width, block_width)
        product = jnp.einsum(
            "rkuv,rkqvy->rkquy", op_block, far_rows, preferred_element_type=jnp.float32
        )
        product = product.astype(jnp.bfloat16)
        term_blocks = jnp.einsum(
            "rpux,rkquy->rpkqxy", own_block, product, preferred_element_type=jnp.float32
        )
        targets = slot_block.reshape(-1)
        local_slot = targets // sub_count * 5 + (targets % sub_count - my_sub + 2)
        window_sums = window_sums + gather_sum(
            local_slot, term_blocks.reshape(-1, block_width, block_width), group_count * 5
        )
        return (window_sums, None)

    start_sums = jnp.zeros((group_count * 5, block_width, block_width), jnp.float32)
    window_sums, _ = lax.scan(advance, start_sums, jnp.arange(block_count))
    window = window_sums.reshape(group_count, 5, block_width, block_width)
    widened = jnp.zeros((group_count, sub_count + 4, block_width, block_width), jnp.float32)
    zero_index = jnp.zeros((), jnp.int32)
    widened = lax.dynamic_update_slice(
        widened, window, (zero_index, my_sub, zero_index, zero_index)
    )
    arranged = widened[:, 2 : 2 + sub_count]
    flat_sums = arranged.reshape(devices, block_width, block_width)
    received = lax.all_to_all(flat_sums, ("group", "sub"), split_axis=0, concat_axis=0, tiled=True)
    summed = gather_sum(recv_block, received, OWN + 1)
    return summed[:OWN]


def solution(mesh):
    return jax.shard_map(
        per_device,
        mesh=mesh,
        in_specs=(
            P(("group", "sub"), None, None, None),
            P(("group", "sub"), None),
            P(("group", "sub"), None, None, None),
            P(("group", "sub")),
            P(("group", "sub"), None, None, None),
            P(("group", "sub")),
        ),
        out_specs=P(("group", "sub"), None, None),
        check_vma=False,
    )
```

profile of v0, /device:TPU:24, one launch (start us, length us, event | category | flops | bytes accessed | tf_op | source)
XLA Modules:
  0.0 405.4 jit_solution(10221041242674332516)
XLA Ops:
  0.0 2.9 convolution_convert_fusion.1
  3.1 1.9 collective-permute-start
  5.1 5.8 %collective-permute-start.1 = (bf16[8,2,128,128]{3,2,1,0:T(8,128)(2,1)S(1)}, bf16[8,2,128,128]{3,2,1,0:T(8,128)(2,1)}, u32[]{:S(2)}, u32[]{:S(2)}) collective-permute-start(bf16[8,2,128,128]{3,2,1,0:T(8,128)(2,1)S(1)} %copy.22), channel_id=1, source_target_pairs={{1,0},{2,1},{3,2},{4,3},{5,4},{6,5},{7,6},{8,7},{9,8},{10,9},{11,1... | collective-permute-start | bytes 1572872 | tf_op jit(solution)/shard_map/ppermute | solution.py:17
  11.0 4.7 %collective-permute-done = bf16[8,2,128,128]{3,2,1,0:T(8,128)(2,1)S(1)} collective-permute-done((bf16[8,2,128,128]{3,2,1,0:T(8,128)(2,1)S(1)}, bf16[8,2,128,128]{3,2,1,0:T(8,128)(2,1)S(1)}, u32[]{:S(2)}, u32[]{:S(2)}) %collective-permute-start) | collective-permute-done | bytes 524320 | tf_op jit(solution)/shard_map/ppermute | solution.py:16
  17.5 2.1 pad_maximum_fusion
  19.7 256.0 %while.13 = (s32[]{:T(128)}, f32[20,128,128]{2,0,1:T(8,128)}, s32[4]{0:T(128)S(1)}, s32[32,2,9,2]{0,3,2,1:T(2,128)S(1)}, s32[]{:T(128)}, /*index=5*/s32[32,9]{1,...) while((s32[]{:T(128)}, f32[20,128,128]{2,0,1:T(8,128)}, ...), condition=%wide.region_1.2_spmd.clone, body=%wide.region_0.1_spmd.clone.sunk | while | flops 3176283648 | bytes 103035632 | solution.py:81
  20.9 2.6 fusion.58
  23.5 3.5 copy.67
  27.0 13.5 %convolution_bitcast_fusion.3 = f32[8,2,9,2,128,128]{4,5,1,3,2,0:T(8,128)} fusion(bf16[8,9,2,128,128]{4,3,2,1,0:T(8,128)(2,1)} %bitcast.97, bf16[32,9,128,128]{3,2,1,0:T(8,128)(2,1)} %get-tuple-element.287, s32[]{:T(128)S(6)} %select_n.61, bf16[32,2,128,128]{3,2,1,0:T(8,128)(2,1)} %get-tuple-element.288), kind=kOutput, calls=%fused_computation.5.clone.1 | convolution fusion | flops 1814298624 | bytes 26477568 | tf_op jit(solution)/shard_map/while/body/eval_jaxpr/rpux,rkquy->rpkqxy/dot_general | solution.py:70
  40.4 18.7 %copy.68 = f32[8,2,9,2,128,128]{5,4,3,2,1,0:T(8,128)} copy(f32[8,2,9,2,128,128]{4,5,1,3,2,0:T(8,128)} %convolution_bitcast_fusion.3) | data formatting | bytes 37748736 | tf_op jit(solution)/shard_map/while/body/eval_jaxpr/rpux,rkquy->rpkqxy/transpose | solution.py:70
  59.6 23.9 %select_add_fusion.2 = f32[20,128,128]{2,0,1:T(8,128)} fusion(f32[20,128,128]{2,0,1:T(8,128)} %get-tuple-element.268, pred[]{:T(512)S(6)} %compare.15, s32[288]{0:T(512)S(1)} %fusion.57, f32[36,8,128,128]{3,2,1,0:T(8,128)} %bitcast.96), kind=kOutput, calls=%fused_computation.14.clone.1 | convolution fusion | flops 1133123200 | bytes 21496960 | tf_op jit(solution)/shard_map/while/body/eval_jaxpr/dot_general | solution.py:31
  84.8 2.6 fusion.58
  87.4 3.5 copy.67
  90.9 13.5 %convolution_bitcast_fusion.3 = f32[8,2,9,2,128,128]{4,5,1,3,2,0:T(8,128)} fusion(bf16[8,9,2,128,128]{4,3,2,1,0:T(8,128)(2,1)} %bitcast.97, bf16[32,9,128,128]{3,2,1,0:T(8,128)(2,1)} %get-tuple-element.287, s32[]{:T(128)S(6)} %select_n.61, bf16[32,2,128,128]{3,2,1,0:T(8,128)(2,1)} %get-tuple-element.288), kind=kOutput, calls=%fused_computation.5.clone.1 | convolution fusion | flops 1814298624 | bytes 26477568 | tf_op jit(solution)/shard_map/while/body/eval_jaxpr/rpux,rkquy->rpkqxy/dot_general | solution.py:70
  104.3 18.7 %copy.68 = f32[8,2,9,2,128,128]{5,4,3,2,1,0:T(8,128)} copy(f32[8,2,9,2,128,128]{4,5,1,3,2,0:T(8,128)} %convolution_bitcast_fusion.3) | data formatting | bytes 37748736 | tf_op jit(solution)/shard_map/while/body/eval_jaxpr/rpux,rkquy->rpkqxy/transpose | solution.py:70
  123.5 24.1 %select_add_fusion.2 = f32[20,128,128]{2,0,1:T(8,128)} fusion(f32[20,128,128]{2,0,1:T(8,128)} %get-tuple-element.268, pred[]{:T(512)S(6)} %compare.15, s32[288]{0:T(512)S(1)} %fusion.57, f32[36,8,128,128]{3,2,1,0:T(8,128)} %bitcast.96), kind=kOutput, calls=%fused_computation.14.clone.1 | convolution fusion | flops 1133123200 | bytes 21496960 | tf_op jit(solution)/shard_map/while/body/eval_jaxpr/dot_general | solution.py:31
  148.8 2.6 fusion.58
  151.4 3.5 copy.67
  154.9 13.5 %convolution_bitcast_fusion.3 = f32[8,2,9,2,128,128]{4,5,1,3,2,0:T(8,128)} fusion(bf16[8,9,2,128,128]{4,3,2,1,0:T(8,128)(2,1)} %bitcast.97, bf16[32,9,128,128]{3,2,1,0:T(8,128)(2,1)} %get-tuple-element.287, s32[]{:T(128)S(6)} %select_n.61, bf16[32,2,128,128]{3,2,1,0:T(8,128)(2,1)} %get-tuple-element.288), kind=kOutput, calls=%fused_computation.5.clone.1 | convolution fusion | flops 1814298624 | bytes 26477568 | tf_op jit(solution)/shard_map/while/body/eval_jaxpr/rpux,rkquy->rpkqxy/dot_general | solution.py:70
  168.4 18.7 %copy.68 = f32[8,2,9,2,128,128]{5,4,3,2,1,0:T(8,128)} copy(f32[8,2,9,2,128,128]{4,5,1,3,2,0:T(8,128)} %convolution_bitcast_fusion.3) | data formatting | bytes 37748736 | tf_op jit(solution)/shard_map/while/body/eval_jaxpr/rpux,rkquy->rpkqxy/transpose | solution.py:70
  187.6 24.1 %select_add_fusion.2 = f32[20,128,128]{2,0,1:T(8,128)} fusion(f32[20,128,128]{2,0,1:T(8,128)} %get-tuple-element.268, pred[]{:T(512)S(6)} %compare.15, s32[288]{0:T(512)S(1)} %fusion.57, f32[36,8,128,128]{3,2,1,0:T(8,128)} %bitcast.96), kind=kOutput, calls=%fused_computation.14.clone.1 | convolution fusion | flops 1133123200 | bytes 21496960 | tf_op jit(solution)/shard_map/while/body/eval_jaxpr/dot_general | solution.py:31
  212.9 2.6 fusion.58
  215.4 3.5 copy.67
  218.9 13.5 %convolution_bitcast_fusion.3 = f32[8,2,9,2,128,128]{4,5,1,3,2,0:T(8,128)} fusion(bf16[8,9,2,128,128]{4,3,2,1,0:T(8,128)(2,1)} %bitcast.97, bf16[32,9,128,128]{3,2,1,0:T(8,128)(2,1)} %get-tuple-element.287, s32[]{:T(128)S(6)} %select_n.61, bf16[32,2,128,128]{3,2,1,0:T(8,128)(2,1)} %get-tuple-element.288), kind=kOutput, calls=%fused_computation.5.clone.1 | convolution fusion | flops 1814298624 | bytes 26477568 | tf_op jit(solution)/shard_map/while/body/eval_jaxpr/rpux,rkquy->rpkqxy/dot_general | solution.py:70
  232.4 18.7 %copy.68 = f32[8,2,9,2,128,128]{5,4,3,2,1,0:T(8,128)} copy(f32[8,2,9,2,128,128]{4,5,1,3,2,0:T(8,128)} %convolution_bitcast_fusion.3) | data formatting | bytes 37748736 | tf_op jit(solution)/shard_map/while/body/eval_jaxpr/rpux,rkquy->rpkqxy/transpose | solution.py:70
  251.6 24.1 %select_add_fusion.2 = f32[20,128,128]{2,0,1:T(8,128)} fusion(f32[20,128,128]{2,0,1:T(8,128)} %get-tuple-element.268, pred[]{:T(512)S(6)} %compare.15, s32[288]{0:T(512)S(1)} %fusion.57, f32[36,8,128,128]{3,2,1,0:T(8,128)} %bitcast.96), kind=kOutput, calls=%fused_computation.14.clone.1 | convolution fusion | flops 1133123200 | bytes 21496960 | tf_op jit(solution)/shard_map/while/body/eval_jaxpr/dot_general | solution.py:31
  275.7 1.7 copy.25
  277.3 1.2 broadcast_in_dim.4
  279.7 107.7 %all_to_all.5 = f32[128,128,128]{2,1,0:T(8,128)} all-to-all(f32[128,128,128]{2,1,0:T(8,128)S(1)} %bitcast.99), channel_id=1, replica_groups=mesh['group'=4,'sub'=32] {'group','sub'}, dimensions={0} | all-to-all | bytes 16777216 | tf_op jit(solution)/shard_map/all_to_all | solution.py:90
  387.4 9.3 %copy.26 = f32[128,128,128]{0,2,1:T(8,128)} copy(f32[128,128,128]{2,1,0:T(8,128)} %all_to_all.5) | data formatting | bytes 16777216 | tf_op jit(solution)/shard_map/all_to_all | solution.py:90
  396.8 6.9 %convolution_bitcast_fusion.1 = f32[4,8,128,128]{3,1,2,0:T(8,128)S(1)} fusion(f32[128,16384]{0,1:T(8,128)} %bitcast.100, s32[128]{0:T(128)S(1)} %copy-done.3), kind=kOutput, calls=%fused_computation.41 | convolution fusion | flops 805314560 | bytes 10486272 | tf_op jit(solution)/shard_map/dot_general | solution.py:31
  403.7 1.7 copy.37
  (45 shorter events, 7.9 us)
Async XLA Ops:
  0.0 10.9 %copy-start.2 = (s32[32,9]{0,1:T(8,128)S(1)}, s32[32,9]{0,1:T(8,128)}, u32[]{:S(2)}) copy-start(s32[32,9]{0,1:T(8,128)} %param.9) | copy-start | bytes 3460
  3.1 12.6 %collective-permute-start = (bf16[8,2,128,128]{3,2,1,0:T(8,128)(2,1)S(1)}, bf16[8,2,128,128]{3,2,1,0:T(8,128)(2,1)S(1)}, u32[]{:S(2)}, u32[]{:S(2)}) collective-permute-start(bf16[8,2,128,128]{3,2,1,0:T(8,128)(2,1)S(1)} %copy.21), channel_id=1, source_target_pairs={{0,1},{1,2},{2,3},{3,4},{4,5},{5,6},{6,7},{7,8},{8,9},{9,10},{10,1... | collective-permute-start | bytes 1572872 | tf_op jit(solution)/shard_map/ppermute | solution.py:16
  5.1 12.4 %collective-permute-start.1 = (bf16[8,2,128,128]{3,2,1,0:T(8,128)(2,1)S(1)}, bf16[8,2,128,128]{3,2,1,0:T(8,128)(2,1)}, u32[]{:S(2)}, u32[]{:S(2)}) collective-permute-start(bf16[8,2,128,128]{3,2,1,0:T(8,128)(2,1)S(1)} %copy.22), channel_id=1, source_target_pairs={{1,0},{2,1},{3,2},{4,3},{5,4},{6,5},{7,6},{8,7},{9,8},{10,9},{11,1... | collective-permute-start | bytes 1572872 | tf_op jit(solution)/shard_map/ppermute | solution.py:17
  11.0 8.7 %copy-start.1 = (s32[32,2,9,2]{0,3,2,1:T(2,128)S(1)}, s32[32,2,9,2]{0,3,2,1:T(2,128)}, u32[]{:S(2)}) copy-start(s32[32,2,9,2]{0,3,2,1:T(2,128)} %param.12) | copy-start | bytes 13828
  15.7 0.8 copy-start
  387.4 9.3 %copy-start.3 = (s32[128]{0:T(128)S(1)}, s32[128]{0:T(128)}, u32[]{:S(2)}) copy-start(s32[128]{0:T(128)} %param.13) | copy-start | bytes 1540
where the time goes:
time: 409 us; the launch traced here: 405 us
  matrix products  170 us (42%)
  local copies, waits for them, and re-layouts  109 us (27%)
  blocking collectives  108 us (26%)
  starting transfers between devices  7.67 us (2%)
  waiting for transfers between devices  5.77 us (1%)
    all_to_all x1, blocking collectives, per_device(): lax.all_to_all(flat_sums, ('group', 'sub'), split_axis=0, concat_axis=0,...  108 us
    dot_general x5, matrix products, gather_sum(): jnp.dot(picker, values.reshape(values.shape[0], -1), precision=lax.Precis...  103 us
    transpose x4, local copies, waits for them, and re-layouts, advance(): jnp.einsum('rpux,rkquy->rpkqxy', own_block, product, preferred_element_ty...  74.9 us
    dot_general x4, matrix products, advance(): jnp.einsum('rpux,rkquy->rpkqxy', own_block, product, preferred_element_ty...  53.8 us
    while x4, local copies, waits for them, and re-layouts  13.9 us
    dot_general x5, matrix products, select_bf(): jnp.dot(picker, table.reshape(count, -1), preferred_element_type=jnp.floa...  13.2 us
    all_to_all x1, local copies, waits for them, and re-layouts, per_device(): lax.all_to_all(flat_sums, ('group', 'sub'), split_axis=0, concat_axis=0,...  9.31 us
  transfers between devices with their start and end apart: 2, of which 2 were waited for; matrix products, arithmetic and copies ran while one was open for 0% of the time, Pallas kernels for 0%

commit v1 on v0

v1 whole, which is shorter than its diff:
```python
import functools

import jax
import jax.numpy as jnp
from jax import lax
from jax.experimental import pallas as pl
from jax.experimental.pallas import tpu as pltpu
from jax.sharding import PartitionSpec as P

B = 128
ROWS = 32
SLOTS_A = 9
SLOTS_P = 2
HALO = 8
OWN = 32
N_GROUP = 4
N_SUB = 32
ENTRIES = ROWS * SLOTS_A
WIN = 5
BUCKETS = N_GROUP * WIN
E = 16
RING = 4
U = 8
G = 8
LIST = ENTRIES * 4 + U
DUMMY = ENTRIES * SLOTS_P
RUNS = ENTRIES * 4 // U + BUCKETS + G
MIB = 2**20
MESH = pl.DeviceIdType.MESH
BF = jnp.bfloat16
F32 = jnp.float32
ANY = pl.BlockSpec(memory_space=pl.ANY)
SMEM = pl.BlockSpec(memory_space=pltpu.SMEM)
VMEM = pl.BlockSpec(memory_space=pltpu.VMEM)


def dot(a, b):
    return jnp.dot(a, b, preferred_element_type=F32)


def pack_kernel(halo_send, p_hbm, to_prev, to_next, sems):
    copies = []
    for j in range(2 * HALO):
        out = (to_prev if j < HALO else to_next).at[j % HALO]
        copies.append(pltpu.make_async_copy(p_hbm.at[halo_send[j]], out, sems.at[j]))
    for copy in copies:
        copy.start()
    for copy in copies:
        copy.wait()


def pack_halo(halo_send, p_vals):
    shape = jax.ShapeDtypeStruct((HALO, SLOTS_P, B, B), BF)
    return pl.pallas_call(
        pack_kernel,
        out_shape=(shape, shape),
        in_specs=[SMEM, ANY],
        out_specs=(ANY, ANY),
        scratch_shapes=[pltpu.SemaphoreType.DMA((2 * HALO,))],
        name="pack_halo",
    )(halo_send, p_vals)


def triple(cols, slots, a_hbm, far, p_t, lists, out, a_v, prod, run, entry_list, term_list, count, last, sems, local, init):
    def fetch_all(group, start):
        place = lax.rem(group, RING)
        for u in range(E):
            copy = pltpu.make_async_copy(a_hbm.at[entry_list[group * E + u]], a_v.at[place, u], sems.at[place])
            copy.start()

    def wait_all(group):
        place = lax.rem(group, RING)
        pltpu.make_async_copy(a_hbm.at[pl.ds(0, E)], a_v.at[place], sems.at[place]).wait()

    def list_body(e, n):
        entry_list[n] = e
        return n + ((cols[e] < ROWS) == local).astype(jnp.int32)

    n_entries = lax.fori_loop(0, ENTRIES, list_body, 0, unroll=8)
    for u in range(E):
        entry_list[n_entries + u] = 0
    groups = (n_entries + E - 1) // E
    for g in range(RING):
        pl.when(g < groups)(functools.partial(fetch_all, g, None))
    for s in range(BUCKETS + 1):
        count[s] = 0
    for u in range(U):
        term_list[BUCKETS, u] = DUMMY
    prod[DUMMY] = jnp.zeros((B, B), BF)
    init()

    @pl.loop(0, groups)
    def _(group):
        wait_all(group)
        place = lax.rem(group, RING)
        for u in range(E):
            j = group * E + u
            e = entry_list[j]
            c = cols[e]
            x = far(c)
            x = jnp.concatenate([x[0], x[1]], axis=1)
            y = dot(a_v[place, u], x).astype(BF)
            prod[j * 2] = y[:, :B]
            prod[j * 2 + 1] = y[:, B:]
        for u in range(E):
            j = group * E + u
            e = entry_list[j]
            i = e // SLOTS_A
            k = e - i * SLOTS_A
            step = (j < n_entries).astype(jnp.int32)
            for p in range(SLOTS_P):
                for q in range(SLOTS_P):
                    s = slots[i * 36 + k * 2 + (p * 18 + q)]
                    n = count[s]
                    term_list[s, n] = (i * 2 + p) * 1024 + (j * 2 + q)
                    count[s] = n + step

        @pl.when(group + RING < groups)
        def _():
            fetch_all(group + RING, None)

    chunks = 0
    for s in range(BUCKETS):
        n = count[s]
        for u in range(U):
            term_list[s, n + u] = DUMMY
        chunks = chunks + jnp.maximum((n + U - 1) // U, 1)

    def step_body(it, carry):
        s, off, acc = carry
        for g in range(G):
            left, right = [], []
            for u in range(U):
                w = term_list[s, off + u]
                left.append(p_t[w >> 10])
                right.append(prod[w & 1023])
            keep = (off > 0).astype(F32)
            acc = acc * keep + dot(jnp.concatenate(left, axis=1), jnp.concatenate(right, axis=0))
            j = it * G + g
            run[j] = acc
            last[s] = j
            off = off + U
            done = off >= count[s]
            off = jnp.where(done, 0, off)
            s = jnp.where(done, jnp.minimum(s + 1, BUCKETS), s)
        return s, off, acc

    lax.fori_loop(0, (chunks + G - 1) // G, step_body, (0, 0, jnp.zeros((B, B), F32)))


def local_kernel(cols, slots, a_hbm, p_hbm, out, pt_out, a_v, p_v, p_t, prod, run, entry_list, term_list, count, last, sems, p_sem, pt_sem):
    load = pltpu.make_async_copy(p_hbm, p_v, p_sem)
    load.start()
    save = pltpu.make_async_copy(p_t, pt_out, pt_sem)

    def init():
        load.wait()

        @pl.loop(0, ROWS)
        def _(i):
            for p in range(SLOTS_P):
                p_t[i * 2 + p] = p_v[i, p].T

        save.start()

    triple(cols, slots, a_hbm, lambda c: p_v[jnp.minimum(c, ROWS - 1)], p_t, None, out, a_v, prod, run, entry_list, term_list, count, last, sems, True, init)
    for s in range(BUCKETS):
        out[s] = run[last[s]]
    save.wait()


def far_kernel(cols, slots, a_hbm, pt_hbm, before, after, acc, out, a_v, h_v, p_t, prod, run, entry_list, term_list, count, last, sems, in_sems):
    loads = [
        pltpu.make_async_copy(before, h_v.at[pl.ds(0, HALO)], in_sems.at[0]),
        pltpu.make_async_copy(after, h_v.at[pl.ds(HALO, HALO)], in_sems.at[1]),
        pltpu.make_async_copy(pt_hbm, p_t, in_sems.at[2]),
    ]
    for load in loads:
        load.start()

    def init():
        for load in loads:
            load.wait()

    triple(cols, slots, a_hbm, lambda c: h_v[jnp.maximum(c - ROWS, 0)], p_t, None, out, a_v, prod, run, entry_list, term_list, count, last, sems, False, init)
    for s in range(BUCKETS):
        out[s] = (acc[s] + run[last[s]]).astype(BF)


def common_scratch():
    return [
        pltpu.VMEM((ENTRIES * 2 + 2 * E + 8, B, B), BF),
        pltpu.VMEM((RUNS, B, B), F32),
        pltpu.SMEM((ENTRIES + E,), jnp.int32),
        pltpu.SMEM((BUCKETS + 1, LIST), jnp.int32),
        pltpu.SMEM((BUCKETS + 1,), jnp.int32),
        pltpu.SMEM((BUCKETS + 1,), jnp.int32),
        pltpu.SemaphoreType.DMA((RING,)),
    ]


def local_terms(cols, slots, a, p_vals):
    return pl.pallas_call(
        local_kernel,
        out_shape=(jax.ShapeDtypeStruct((BUCKETS, B, B), F32), jax.ShapeDtypeStruct((ROWS * 2, B, B), BF)),
        in_specs=[SMEM, SMEM, ANY, ANY],
        out_specs=(VMEM, ANY),
        scratch_shapes=[
            pltpu.VMEM((RING, E, B, B), BF),
            pltpu.VMEM((ROWS, SLOTS_P, B, B), BF),
            pltpu.VMEM((ROWS * 2, B, B), BF),
        ]
        + common_scratch()
        + [pltpu.SemaphoreType.DMA, pltpu.SemaphoreType.DMA],
        compiler_params=pltpu.CompilerParams(vmem_limit_bytes=56 * MIB),
        cost_estimate=pl.CostEstimate(flops=6 * 10**9, bytes_accessed=30 * 10**6, transcendentals=0),
        name="local_terms",
    )(cols, slots, a, p_vals)


def far_terms(cols, slots, a, p_t, before, after, acc):
    return pl.pallas_call(
        far_kernel,
        out_shape=jax.ShapeDtypeStruct((BUCKETS, B, B), BF),
        in_specs=[SMEM, SMEM, ANY, ANY, ANY, ANY, VMEM],
        out_specs=VMEM,
        scratch_shapes=[
            pltpu.VMEM((RING, E, B, B), BF),
            pltpu.VMEM((2 * HALO, SLOTS_P, B, B), BF),
            pltpu.VMEM((ROWS * 2, B, B), BF),
        ]
        + common_scratch()
        + [pltpu.SemaphoreType.DMA((3,))],
        compiler_params=pltpu.CompilerParams(vmem_limit_bytes=56 * MIB),
        name="far_terms",
    )(cols, slots, a, p_t, before, after, acc)


def exchange_kernel(partial, received, send_sems, recv_sems, own_sem):
    g = lax.axis_index("group")
    s = lax.axis_index("sub")
    peers = []
    for dg in (2, 1, 3, 0):
        for off in range(-2, 3):
            if dg or off:
                peers.append((dg, off, lax.rem(g + dg, N_GROUP), lax.rem(s + (off + N_SUB), N_SUB)))
    barrier = pltpu.get_barrier_semaphore()
    for _, _, tg, ts in peers:
        pl.semaphore_signal(barrier, inc=1, device_id=(tg, ts), device_id_type=MESH)
    own = pltpu.make_async_copy(partial.at[g * WIN + 2], received.at[2], own_sem)
    own.start()
    pl.semaphore_wait(barrier, len(peers))
    copies = []
    for dg, off, tg, ts in peers:
        j = dg * WIN + off + 2
        copy = pltpu.make_async_remote_copy(
            src_ref=partial.at[tg * WIN + (off + 2)],
            dst_ref=received.at[j],
            send_sem=send_sems.at[j],
            recv_sem=recv_sems.at[j],
            device_id=(tg, ts),
            device_id_type=MESH,
        )
        copy.start()
        copies.append(copy)
    own.wait()
    for copy in copies:
        copy.wait()


def exchange(partial):
    return pl.pallas_call(
        exchange_kernel,
        out_shape=jax.ShapeDtypeStruct((BUCKETS, B, B), BF),
        in_specs=[ANY],
        out_specs=ANY,
        scratch_shapes=[
            pltpu.SemaphoreType.DMA((BUCKETS,)),
            pltpu.SemaphoreType.DMA((BUCKETS,)),
            pltpu.SemaphoreType.DMA,
        ],
        compiler_params=pltpu.CompilerParams(collective_id=0, has_side_effects=True),
        name="exchange",
    )(partial)


def place_kernel(targets, received, out):
    g = lax.axis_index("group")
    s = lax.axis_index("sub")
    out[...] = jnp.zeros_like(out)
    for dg in range(N_GROUP):
        for off in range(-2, 3):
            sg = lax.rem(g - dg + N_GROUP, N_GROUP)
            ss = s - off
            inside = jnp.logical_and(ss >= 0, ss < N_SUB)
            o = targets[jnp.where(inside, sg * N_SUB + ss, 0)]

            @pl.when(jnp.logical_and(inside, o < OWN))
            def _():
                out[o] += received[dg * WIN + off + 2].astype(F32)


def place(targets, received):
    return pl.pallas_call(
        place_kernel,
        out_shape=jax.ShapeDtypeStruct((OWN, B, B), F32),
        in_specs=[SMEM, VMEM],
        out_specs=VMEM,
        name="place",
    )(targets, received)


def per_device(a_vals, a_cols, p_vals, halo_send, send_slot, recv_block):
    my_sub = lax.axis_index("sub")
    to_prev, to_next = pack_halo(halo_send, p_vals)
    up = [(i, i + 1) for i in range(N_SUB - 1)]
    down = [(j, i) for i, j in up]
    before = lax.ppermute(to_next, "sub", up)
    after = lax.ppermute(to_prev, "sub", down)
    cols = a_cols.reshape(-1)
    flat = send_slot.reshape(-1)
    slots = flat // N_SUB * WIN + (flat % N_SUB - my_sub + 2)
    a = a_vals.reshape(ENTRIES, B, B)
    acc, p_t = local_terms(cols, slots, a, p_vals)
    partial = far_terms(cols, slots, a, p_t, before, after, acc)
    received = exchange(partial)
    return place(recv_block, received)


def solution(mesh):
    return jax.shard_map(
        per_device,
        mesh=mesh,
        in_specs=(
            P(("group", "sub"), None, None, None),
            P(("group", "sub"), None),
            P(("group", "sub"), None, None, None),
            P(("group", "sub")),
            P(("group", "sub"), None, None, None),
            P(("group", "sub")),
        ),
        out_specs=P(("group", "sub"), None, None),
        check_vma=False,
    )
```

time: 409 us -> 106 us (0.26)
  the two profiles are of different devices: /device:TPU:24 before, /device:TPU:1 now
where the time goes in v1:
time: 106 us; the launch traced here: 105 us
  Pallas kernels  95.4 us (90%)
  starting transfers between devices  6.86 us (6%)
  local copies, waits for them, and re-layouts  2.42 us (2%)
    pallas_call x1, Pallas kernels, pack_halo(): pl.pallas_call(pack_kernel, out_shape=(shape, shape), in_specs=[SMEM, ANY...  33.8 us
    pallas_call x1, Pallas kernels, local_terms(): pl.pallas_call(local_kernel, out_shape=(jax.ShapeDtypeStruct((BUCKETS, B,...  24.1 us
    pallas_call x1, Pallas kernels, exchange(): pl.pallas_call(exchange_kernel, out_shape=jax.ShapeDtypeStruct((BUCKETS,...  19.2 us
    pallas_call x1, Pallas kernels, far_terms(): pl.pallas_call(far_kernel, out_shape=jax.ShapeDtypeStruct((BUCKETS, B, B)...  15.5 us
    ppermute x1, starting transfers between devices, per_device(): before = lax.ppermute(to_next, 'sub', up)  4.94 us
    pallas_call x1, Pallas kernels, place(): pl.pallas_call(place_kernel, out_shape=jax.ShapeDtypeStruct((OWN, B, B),...  2.81 us
  transfers between devices with their start and end apart: 2, of which 0 were waited for; matrix products, arithmetic and copies ran while one was open for 2% of the time, Pallas kernels for 23%

profile of v1, /device:TPU:1, one launch (start us, length us, event | category | flops | bytes accessed | tf_op | source)
XLA Modules:
  0.0 105.4 jit_solution(3800455247444871364)
XLA Ops:
  0.0 0.0 copy-start.3
  0.0 0.0 copy-start.2
  0.0 33.8 %pack_halo.1 = (bf16[8,2,128,128]{3,2,1,0:T(8,128)(2,1)}, bf16[8,2,128,128]{3,2,1,0:T(8,128)(2,1)}) custom-call(s32[16]{0:T(128)} %halo_send.1, bf16[32,2,128,128]{3,2,1,0:T(8,128)(2,1)} %p_hbm.3), custom_call_target="tpu_custom_call" | custom-call | tf_op jit(solution)/shard_map/pack_halo/pallas_call | solution.py:54
  33.8 4.9 %collective-permute-start = (bf16[8,2,128,128]{3,2,1,0:T(8,128)(2,1)}, bf16[8,2,128,128]{3,2,1,0:T(8,128)(2,1)S(1)}, u32[]{:S(2)}, u32[]{:S(2)}) collective-permute-start(bf16[8,2,128,128]{3,2,1,0:T(8,128)(2,1)} %get-tuple-element.10), channel_id=1, source_target_pairs={{0,1},{1,2},{2,3},{3,4},{4,5},{5,6},{6,7},{7,8},{8,9},{9,10},{10,1... | collective-permute-start | bytes 1572872 | tf_op jit(solution)/shard_map/ppermute | solution.py:318
  38.8 1.9 %collective-permute-start.1 = (bf16[8,2,128,128]{3,2,1,0:T(8,128)(2,1)}, bf16[8,2,128,128]{3,2,1,0:T(8,128)(2,1)S(1)}, u32[]{:S(2)}, u32[]{:S(2)}) collective-permute-start(bf16[8,2,128,128]{3,2,1,0:T(8,128)(2,1)} %get-tuple-element.11), channel_id=1, source_target_pairs={{1,0},{2,1},{3,2},{4,3},{5,4},{6,5},{7,6},{8,7},{9,8},{10,9},{11,1... | collective-permute-start | bytes 1572872 | tf_op jit(solution)/shard_map/ppermute | solution.py:319
  40.7 0.0 copy-done.3
  40.7 0.1 copy.7
  40.8 0.7 reshape.9.cols
  41.5 0.0 copy-done.2
  41.5 0.5 copy.8
  42.0 0.2 reshape.10
  42.2 0.6 fusion.1.slots
  42.8 24.1 %local_terms.1 = (f32[20,128,128]{2,1,0:T(8,128)}, bf16[64,128,128]{2,1,0:T(8,128)(2,1)}) custom-call(s32[288]{0:T(512)} %reshape.9.cols, s32[1152]{0:T(1024)} %fusion.1.slots, bf16[288,128,128]{2,1,0:T(8,128)(2,1)} %bitcast.1, bf16[32,2,128,128]{3,2,1,0:T(8,128)(2,1)} %p_hbm.3), custom_call_target="tpu_custom_call" | custom-call | flops 6000000000 | bytes 30000000 | tf_op jit(solution)/shard_map/local_terms/pallas_call | solution.py:203
  66.9 0.0 collective-permute-done.before
  66.9 0.0 copy-start
  66.9 0.0 collective-permute-done.1.after
  66.9 0.0 copy-start.1
  66.9 0.8 copy-done
  67.7 0.2 copy-done.1
  67.9 15.5 %far_terms.1.partial = bf16[20,128,128]{2,1,0:T(8,128)(2,1)} custom-call(s32[288]{0:T(512)} %reshape.9.cols, s32[1152]{0:T(1024)} %fusion.1.slots, bf16[288,128,128]{2,1,0:T(8,128)(2,1)} %bitcast.2, bf16[64,128,128]{2,1,0:T(8,128)(2,1)} %get-tuple-element.9.pt_hbm, bf16[8,2,128,128]{3,2,1,0:T(8,128)(2,1)} %copy-done, bf16[8,2,128,128]{3,2,1,0:T(8,128)(2,1)} %copy-done.1, ...), custom_call_target="tpu_custom_call" | custom-call | tf_op jit(solution)/shard_map/far_terms/pallas_call | solution.py:222
  83.3 19.2 %exchange.1.received = bf16[20,128,128]{2,1,0:T(8,128)(2,1)} custom-call(bf16[20,128,128]{2,1,0:T(8,128)(2,1)} %far_terms.1.partial), custom_call_target="tpu_custom_call" | custom-call | tf_op jit(solution)/shard_map/exchange/pallas_call | solution.py:272
  102.6 2.8 %place.1 = f32[32,128,128]{2,1,0:T(8,128)} custom-call(s32[128]{0:T(128)} %targets.1, bf16[20,128,128]{2,1,0:T(8,128)(2,1)} %exchange.1.received), custom_call_target="tpu_custom_call" | custom-call | tf_op jit(solution)/shard_map/place/pallas_call | solution.py:304
Async XLA Ops:
  0.0 40.7 %copy-start.3 = (s32[32,9]{0,1:T(8,128)S(1)}, s32[32,9]{0,1:T(8,128)}, u32[]{:S(2)}) copy-start(s32[32,9]{0,1:T(8,128)} %param.7) | copy-start | bytes 3460
  0.0 41.5 %copy-start.2 = (s32[32,2,9,2]{0,3,2,1:T(2,128)S(1)}, s32[32,2,9,2]{0,3,2,1:T(2,128)}, u32[]{:S(2)}) copy-start(s32[32,2,9,2]{0,3,2,1:T(2,128)} %param.10) | copy-start | bytes 13828
  33.8 33.0 %collective-permute-start = (bf16[8,2,128,128]{3,2,1,0:T(8,128)(2,1)}, bf16[8,2,128,128]{3,2,1,0:T(8,128)(2,1)S(1)}, u32[]{:S(2)}, u32[]{:S(2)}) collective-permute-start(bf16[8,2,128,128]{3,2,1,0:T(8,128)(2,1)} %get-tuple-element.10), channel_id=1, source_target_pairs={{0,1},{1,2},{2,3},{3,4},{4,5},{5,6},{6,7},{7,8},{8,9},{9,10},{10,1... | collective-permute-start | bytes 1572872 | tf_op jit(solution)/shard_map/ppermute | solution.py:318
  38.8 28.1 %collective-permute-start.1 = (bf16[8,2,128,128]{3,2,1,0:T(8,128)(2,1)}, bf16[8,2,128,128]{3,2,1,0:T(8,128)(2,1)S(1)}, u32[]{:S(2)}, u32[]{:S(2)}) collective-permute-start(bf16[8,2,128,128]{3,2,1,0:T(8,128)(2,1)} %get-tuple-element.11), channel_id=1, source_target_pairs={{1,0},{2,1},{3,2},{4,3},{5,4},{6,5},{7,6},{8,7},{9,8},{10,9},{11,1... | collective-permute-start | bytes 1572872 | tf_op jit(solution)/shard_map/ppermute | solution.py:319
  66.9 0.8 copy-start
  66.9 1.0 copy-start.1

commit v2 on v0

v2 whole, which is shorter than its diff:
```python
import functools

import jax
import jax.numpy as jnp
from jax import lax
from jax.experimental import pallas as pl
from jax.experimental.pallas import tpu as pltpu
from jax.sharding import PartitionSpec as P

B = 128
ROWS = 32
SLOTS_A = 9
SLOTS_P = 2
HALO = 8
OWN = 32
N_GROUP = 4
N_SUB = 32
ENTRIES = ROWS * SLOTS_A
TERMS = ENTRIES * 4
WIN = 5
BUCKETS = N_GROUP * WIN
ROW_RING = 8
ROW_STEP = 2
E = 16
RING = 4
U = 8
G = 8
CHUNKS = 168
PRODS = 2 * ENTRIES + 8
WORD_ROWS = 16
TABLE_ROWS = 24
MIB = 2**20
MESH = pl.DeviceIdType.MESH
BF = jnp.bfloat16
F32 = jnp.float32
SMEM = pl.BlockSpec(memory_space=pltpu.SMEM)
VMEM = pl.BlockSpec(memory_space=pltpu.VMEM)
HBM = pl.BlockSpec(memory_space=pltpu.HBM)


def in_hbm(x):
    return pltpu.with_memory_space_constraint(x, pltpu.HBM)


def in_vmem(x):
    return pltpu.with_memory_space_constraint(x, pltpu.VMEM)


def dot(a, b):
    return jnp.dot(a, b, preferred_element_type=F32)


def product(a, x):
    return dot(a, jnp.concatenate([x[0], x[1]], axis=1)).astype(BF)


def own_kernel(cols, halo_send, a_hbm, p_hbm, prods, p_t, halo, a_v, p_v, packed, a_sems, p_sem, send_sems, recv_sems):
    g = lax.axis_index("group")
    s = lax.axis_index("sub")
    before = (g, lax.rem(s + (N_SUB - 1), N_SUB))
    after = (g, lax.rem(s + 1, N_SUB))
    barrier = pltpu.get_barrier_semaphore()
    for peer in (before, after):
        pl.semaphore_signal(barrier, inc=1, device_id=peer, device_id_type=MESH)
    load = pltpu.make_async_copy(p_hbm, p_v, p_sem)
    load.start()

    def fetch(i):
        place = lax.rem(i, ROW_RING)
        return pltpu.make_async_copy(a_hbm.at[i], a_v.at[place], a_sems.at[place])

    for i in range(ROW_RING):
        fetch(i).start()
    load.wait()
    for j in range(2 * HALO):
        packed[j] = p_v[halo_send[j]]
    pl.semaphore_wait(barrier, 2)
    copies = [
        pltpu.make_async_remote_copy(
            src_ref=packed.at[pl.ds(src, HALO)],
            dst_ref=halo.at[pl.ds(HALO - src, HALO)],
            send_sem=send_sems.at[n],
            recv_sem=recv_sems.at[n],
            device_id=peer,
            device_id_type=MESH,
        )
        for n, (src, peer) in enumerate(((0, before), (HALO, after)))
    ]
    for copy in copies:
        copy.start()
    for j in range(2):
        prods[j] = jnp.zeros((B, B), BF)

    @pl.loop(0, ROWS // ROW_STEP)
    def _(step):
        for r in range(ROW_STEP):
            fetch(step * ROW_STEP + r).wait()
        for r in range(ROW_STEP):
            i = step * ROW_STEP + r
            place = lax.rem(i, ROW_RING)
            for k in range(SLOTS_A):
                e = i * SLOTS_A + k
                y = product(a_v[place, k], p_v[jnp.minimum(cols[e], ROWS - 1)])
                prods[e * 2 + 2] = y[:, :B]
                prods[e * 2 + 3] = y[:, B:]
            for p in range(SLOTS_P):
                p_t[i * 2 + p] = p_v[i, p].T
        for r in range(ROW_STEP):
            i = step * ROW_STEP + r + ROW_RING

            @pl.when(i < ROWS)
            def _():
                fetch(i).start()

    for copy in copies:
        copy.wait()

    @pl.when(s == 0)
    def _():
        halo[pl.ds(0, HALO)] = jnp.zeros((HALO, SLOTS_P, B, B), BF)

    @pl.when(s == N_SUB - 1)
    def _():
        halo[pl.ds(HALO, HALO)] = jnp.zeros((HALO, SLOTS_P, B, B), BF)


def own_products(cols, halo_send, a_vals, p_vals):
    return pl.pallas_call(
        own_kernel,
        out_shape=(
            pltpu.VMEM((PRODS, B, B), BF),
            pltpu.VMEM((2 * ROWS, B, B), BF),
            pltpu.VMEM((2 * HALO, SLOTS_P, B, B), BF),
        ),
        in_specs=[SMEM, SMEM, HBM, HBM],
        out_specs=(VMEM, VMEM, VMEM),
        scratch_shapes=[
            pltpu.VMEM((ROW_RING, SLOTS_A, B, B), BF),
            pltpu.VMEM((ROWS, SLOTS_P, B, B), BF),
            pltpu.VMEM((2 * HALO, SLOTS_P, B, B), BF),
            pltpu.SemaphoreType.DMA((ROW_RING,)),
            pltpu.SemaphoreType.DMA,
            pltpu.SemaphoreType.DMA((2,)),
            pltpu.SemaphoreType.DMA((2,)),
        ],
        compiler_params=pltpu.CompilerParams(collective_id=0, has_side_effects=True, vmem_limit_bytes=8 * MIB),
        name="own_products",
    )(cols, halo_send, in_hbm(a_vals), in_hbm(p_vals))


def iota(shape, axis):
    return lax.broadcasted_iota(jnp.int32, shape, axis)


def build_table(slots, table):
    rows = TERMS // B
    width = 32
    one_hot = [
        (jnp.broadcast_to(slots[r : r + 1, :], (width, B)) == iota((width, B), 0)).astype(F32) for r in range(rows)
    ]
    stacked = jnp.concatenate(one_hot, axis=0).astype(BF)
    upper = (iota((B, B), 0) < iota((B, B), 1)).astype(F32).astype(BF)
    rank = dot(stacked, upper)
    total = dot(stacked, jnp.ones((B, B), BF))
    base = jnp.zeros((width, B), F32)
    ranks = []
    for r in range(rows):
        ranks.append(base + rank[r * width : (r + 1) * width])
        base = base + total[r * width : (r + 1) * width]
    bucket = iota((width, B), 0)
    used = ((base.astype(jnp.int32) + (U - 1)) >> 3).astype(F32)
    used = jnp.where(bucket < BUCKETS, jnp.maximum(used, 1.0), 0.0)
    lower = (iota((width, width), 1) < iota((width, width), 0)).astype(F32).astype(BF)
    first = dot(lower, used.astype(BF))
    words = jnp.zeros((3 * WORD_ROWS, B), F32)
    lane = iota((1, B), 1)
    for r in range(rows):
        pos = jnp.sum(one_hot[r] * (first * float(U) + ranks[r]), axis=0, keepdims=True).astype(jnp.int32)
        term = lane + r * B
        i = (term * 1821) >> 16
        rest = term - i * 36
        p = (rest >= 18).astype(jnp.int32)
        block = i * 18 + (rest - p * 18) + 2
        here = jnp.broadcast_to(pos >> 7, (WORD_ROWS, B)) == iota((WORD_ROWS, B), 0)
        parts = [
            jnp.where(here, jnp.broadcast_to(v.astype(F32), (WORD_ROWS, B)), 0.0)
            for v in (i * 2 + p, block >> 4, block & 15)
        ]
        low = (jnp.broadcast_to(pos & (B - 1), (B, B)) == iota((B, B), 0)).astype(F32).astype(BF)
        words = words + lax.dot_general(
            jnp.concatenate(parts, axis=0).astype(BF),
            low,
            (((1,), (1,)), ((), ())),
            preferred_element_type=F32,
        )
    words = words.astype(jnp.int32)
    table[0:WORD_ROWS, :] = words[:WORD_ROWS] * 1024 + words[WORD_ROWS : 2 * WORD_ROWS] * 16 + words[2 * WORD_ROWS :]
    lane32 = iota((width, B), 1).astype(F32)
    starts = jnp.where(bucket < BUCKETS, first, -1.0)
    keep = [1.0 - jnp.sum((starts == lane32 + float(h * B)).astype(F32), axis=0, keepdims=True) for h in range(2)]
    last = jnp.sum(jnp.where(bucket == iota((width, B), 1), first + used - 1.0, 0.0), axis=0, keepdims=True)
    rest = jnp.concatenate(keep + [last, jnp.zeros((5, B), F32)], axis=0)
    table[WORD_ROWS:TABLE_ROWS, :] = rest.astype(jnp.int32)


def far_kernel(cols, slots, a_hbm, halo, _, prods, table, a_v, entry_list, a_sems):
    def fetch(group):
        place = lax.rem(group, RING)
        for u in range(E):
            pltpu.make_async_copy(a_hbm.at[entry_list[group * E + u]], a_v.at[place, u], a_sems.at[place]).start()

    def fetched(group):
        place = lax.rem(group, RING)
        pltpu.make_async_copy(a_hbm.at[pl.ds(0, E)], a_v.at[place], a_sems.at[place]).wait()

    def list_body(e, n):
        entry_list[n] = e
        return n + (cols[e] >= ROWS).astype(jnp.int32)

    entries = lax.fori_loop(0, ENTRIES, list_body, 0, unroll=16)
    groups = (entries + (E - 1)) // E

    @pl.when(entries > 0)
    def _():
        tail = entry_list[entries - 1]
        for u in range(E):
            entry_list[entries + u] = tail

    for group in range(RING):
        pl.when(group < groups)(functools.partial(fetch, group))
    build_table(slots, table)

    @pl.loop(0, groups)
    def _(group):
        place = lax.rem(group, RING)
        fetched(group)

        for u in range(E):
            e = entry_list[group * E + u]
            y = product(a_v[place, u], halo[cols[e] - ROWS])
            prods[e * 2 + 2] = y[:, :B]
            prods[e * 2 + 3] = y[:, B:]

        @pl.when(group + RING < groups)
        def _():
            fetch(group + RING)


def far_products(cols, slots, a, halo, prods):
    return pl.pallas_call(
        far_kernel,
        out_shape=(
            pltpu.VMEM((PRODS, B, B), BF),
            jax.ShapeDtypeStruct((TABLE_ROWS, B), jnp.int32),
        ),
        in_specs=[SMEM, VMEM, HBM, VMEM, VMEM],
        out_specs=(VMEM, VMEM),
        scratch_shapes=[
            pltpu.VMEM((RING, E, B, B), BF),
            pltpu.SMEM((ENTRIES + E,), jnp.int32),
            pltpu.SemaphoreType.DMA((RING,)),
        ],
        input_output_aliases={4: 0},
        compiler_params=pltpu.CompilerParams(vmem_limit_bytes=12 * MIB),
        name="far_products",
    )(cols, slots, in_hbm(a), in_vmem(halo), in_vmem(prods))


def term_kernel(table, prods, p_t, received, run, partial, send_sems, recv_sems):
    g = lax.axis_index("group")
    s = lax.axis_index("sub")
    peers = []
    for dg in (2, 1, 3, 0):
        for off in range(-2, 3):
            if dg or off:
                peers.append((dg, off, lax.rem(g + dg, N_GROUP), lax.rem(s + (off + N_SUB), N_SUB)))
    barrier = pltpu.get_barrier_semaphore()
    for _, _, tg, ts in peers:
        pl.semaphore_signal(barrier, inc=1, device_id=(tg, ts), device_id_type=MESH)

    def step(it, acc):
        for n in range(G):
            c = it * G + n
            left, right = [], []
            for u in range(U):
                w = table[c * U + u]
                left.append(p_t[w >> 10])
                right.append(prods[w & 1023])
            keep = table[WORD_ROWS * B + c].astype(F32)
            acc = acc * keep + dot(jnp.concatenate(left, axis=1), jnp.concatenate(right, axis=0))
            run[c] = acc
        return acc

    lax.fori_loop(0, CHUNKS // G, step, jnp.zeros((B, B), F32))
    pl.semaphore_wait(barrier, len(peers))
    copies = []
    for dg, off, tg, ts in peers:
        j = dg * WIN + off + 2
        partial[j] = run[table[(WORD_ROWS + 2) * B + tg * WIN + (off + 2)]].astype(BF)
        copy = pltpu.make_async_remote_copy(
            src_ref=partial.at[j],
            dst_ref=received.at[j],
            send_sem=send_sems.at[j],
            recv_sem=recv_sems.at[j],
            device_id=(tg, ts),
            device_id_type=MESH,
        )
        copy.start()
        copies.append(copy)
    received[2] = run[table[(WORD_ROWS + 2) * B + g * WIN + 2]].astype(BF)
    for copy in copies:
        copy.wait()


def send_terms(table, prods, p_t):
    return pl.pallas_call(
        term_kernel,
        out_shape=jax.ShapeDtypeStruct((BUCKETS, B, B), BF),
        in_specs=[SMEM, VMEM, VMEM],
        out_specs=VMEM,
        scratch_shapes=[
            pltpu.VMEM((CHUNKS, B, B), F32),
            pltpu.VMEM((BUCKETS, B, B), BF),
            pltpu.SemaphoreType.DMA((BUCKETS,)),
            pltpu.SemaphoreType.DMA((BUCKETS,)),
        ],
        compiler_params=pltpu.CompilerParams(collective_id=1, has_side_effects=True, vmem_limit_bytes=16 * MIB),
        name="send_terms",
    )(table, in_vmem(prods), in_vmem(p_t))


def place_kernel(targets, received, out):
    g = lax.axis_index("group")
    s = lax.axis_index("sub")
    out[...] = jnp.zeros_like(out)
    for dg in range(N_GROUP):
        for off in range(-2, 3):
            sg = lax.rem(g - dg + N_GROUP, N_GROUP)
            ss = s - off
            inside = jnp.logical_and(ss >= 0, ss < N_SUB)
            o = targets[jnp.where(inside, sg * N_SUB + ss, 0)]

            @pl.when(jnp.logical_and(inside, o < OWN))
            def _():
                out[o] += received[dg * WIN + off + 2].astype(F32)


def place(targets, received):
    return pl.pallas_call(
        place_kernel,
        out_shape=jax.ShapeDtypeStruct((OWN, B, B), F32),
        in_specs=[SMEM, VMEM],
        out_specs=VMEM,
        name="place",
    )(targets, in_vmem(received))


def per_device(a_vals, a_cols, p_vals, halo_send, send_slot, recv_block):
    my_sub = lax.axis_index("sub")
    cols = a_cols.reshape(-1)
    prods, p_t, halo = own_products(cols, halo_send, a_vals, p_vals)
    flat = send_slot.reshape(TERMS // B, B)
    slots = flat // N_SUB * WIN + (flat % N_SUB - my_sub + 2)
    prods, table = far_products(cols, slots, a_vals.reshape(ENTRIES, B, B), halo, prods)
    received = send_terms(table.reshape(-1), prods, p_t)
    return place(recv_block, received)


def solution(mesh):
    return jax.shard_map(
        per_device,
        mesh=mesh,
        in_specs=(
            P(("group", "sub"), None, None, None),
            P(("group", "sub"), None),
            P(("group", "sub"), None, None, None),
            P(("group", "sub")),
            P(("group", "sub"), None, None, None),
            P(("group", "sub")),
        ),
        out_specs=P(("group", "sub"), None, None),
        check_vma=False,
    )
```

time: 409 us -> 56.8 us (0.14)
  the two profiles are of different devices: /device:TPU:24 before, /device:TPU:1 now
where the time goes in v2:
time: 56.8 us; the launch traced here: 56.3 us
  Pallas kernels  53.3 us (94%)
  local copies, waits for them, and re-layouts  2.99 us (5%)
    pallas_call x1, Pallas kernels, send_terms(): pl.pallas_call(term_kernel, out_shape=jax.ShapeDtypeStruct((BUCKETS, B, B...  32.2 us
    pallas_call x1, Pallas kernels, own_products(): pl.pallas_call(own_kernel, out_shape=(pltpu.VMEM((PRODS, B, B), BF), pltp...  13.2 us
    pallas_call x1, Pallas kernels, far_products(): pl.pallas_call(far_kernel, out_shape=(pltpu.VMEM((PRODS, B, B), BF), jax....  5.53 us
    unnamed x4, local copies, waits for them, and re-layouts  2.69 us
    pallas_call x1, Pallas kernels, place(): pl.pallas_call(place_kernel, out_shape=jax.ShapeDtypeStruct((OWN, B, B),...  2.38 us

profile of v2, /device:TPU:1, one launch (start us, length us, event | category | flops | bytes accessed | tf_op | source)
XLA Modules:
  0.0 56.3 jit_solution(8295086461186284760)
XLA Ops:
  0.0 0.8 %copy.9 = s32[32,9]{1,0:T(8,128)S(1)} copy(s32[32,9]{0,1:T(8,128)} %param.7) | data formatting | bytes 2304 | tf_op args[1]
  0.8 0.1 reshape.12.cols
  0.9 1.3 %copy.10 = s32[32,2,9,2]{3,2,1,0:T(8,128)S(1)} copy(s32[32,2,9,2]{0,3,2,1:T(2,128)} %param.10) | data formatting | bytes 9216 | tf_op args[4]
  2.2 0.2 reshape.13
  2.4 0.0 copy-start
  2.4 0.6 %copy-done = s32[16]{0:T(128)S(1)} copy-done((s32[16]{0:T(128)S(1)}, s32[16]{0:T(128)}, u32[]{:S(2)}) %copy-start) | copy-done | bytes 88
  3.0 13.2 %own_products.1 = (bf16[584,128,128]{2,1,0:T(8,128)(2,1)S(1)}, bf16[64,128,128]{2,1,0:T(8,128)(2,1)S(1)}, bf16[16,2,128,128]{3,2,1,0:T(8,128)(2,1)S(1)}) custom-call(s32[288]{0:T(512)S(1)} %reshape.12.cols, s32[16]{0:T(128)S(1)} %copy-done, bf16[32,9,128,128]{3,2,1,0:T(8,128)(2,1)} %a_hbm.1, bf16[32,2,128,128]{3,2,1,0:T(8,128)(2,1)} %p_hbm.1), custom_call_target="tpu_custom_call" | custom-call | tf_op jit(solution)/shard_map/own_products/pallas_call | solution.py:128
  16.2 5.5 %far_products.1 = (bf16[584,128,128]{2,1,0:T(8,128)(2,1)S(1)}, s32[24,128]{1,0:T(8,128)S(1)}) custom-call(s32[288]{0:T(512)S(1)} %reshape.12.cols, s32[9,128]{1,0:T(8,128)S(1)} %fusion.1.slots, bf16[288,128,128]{2,1,0:T(8,128)(2,1)} %bitcast.3, bf16[16,2,128,128]{3,2,1,0:T(8,128)(2,1)S(1)} %get-tuple-element.10.halo, ...), custom_call_target="tpu_custom_call", output_to_operand_aliasing={{0}: (4, {})} | custom-call | tf_op jit(solution)/shard_map/far_products/pallas_call | solution.py:250
  21.8 32.2 %send_terms.1.received = bf16[20,128,128]{2,1,0:T(8,128)(2,1)S(1)} custom-call(s32[3072]{0:T(1024)S(1)} %bitcast.2, bf16[584,128,128]{2,1,0:T(8,128)(2,1)S(1)} %get-tuple-element.13.prods, bf16[64,128,128]{2,1,0:T(8,128)(2,1)S(1)} %get-tuple-element.14.p_t), custom_call_target="tpu_custom_call" | custom-call | tf_op jit(solution)/shard_map/send_terms/pallas_call | solution.py:316
  54.0 2.4 %place.1 = f32[32,128,128]{2,1,0:T(8,128)} custom-call(s32[128]{0:T(128)} %targets.1, bf16[20,128,128]{2,1,0:T(8,128)(2,1)S(1)} %send_terms.1.received), custom_call_target="tpu_custom_call" | custom-call | tf_op jit(solution)/shard_map/place/pallas_call | solution.py:349
  (1 shorter events, 0.0 us)
Async XLA Ops:
  2.4 0.7 %copy-start = (s32[16]{0:T(128)S(1)}, s32[16]{0:T(128)}, u32[]{:S(2)}) copy-start(s32[16]{0:T(128)} %halo_send.1) | copy-start | bytes 196

commit v3 on v0

v3 whole, which is shorter than its diff:
```python
import functools

import jax
import jax.numpy as jnp
from jax import lax
from jax.experimental import pallas as pl
from jax.experimental.pallas import tpu as pltpu
from jax.sharding import PartitionSpec as P

B = 128
ROWS = 32
SLOTS_A = 9
SLOTS_P = 2
HALO = 8
OWN = 32
N_GROUP = 4
N_SUB = 32
ENTRIES = ROWS * SLOTS_A
TERMS = ENTRIES * 4
WIN = 5
BUCKETS = N_GROUP * WIN
ROW_RING = 16
ROW_STEP = 4
U = 4
G = 77
CHUNKS = 308
LEFTS = 2 * ENTRIES + 8
OWN_BLOCKS = ROWS * SLOTS_P
FAR_BLOCKS = 2 * HALO * SLOTS_P
WIDTH = 32
WORD_ROWS = 16
KEEP_ROWS = 3
TABLE_ROWS = 24
CODE = 32767.0
MIB = 2**20
MESH = pl.DeviceIdType.MESH
BF = jnp.bfloat16
F32 = jnp.float32
I16 = jnp.int16
SMEM = pl.BlockSpec(memory_space=pltpu.SMEM)
VMEM = pl.BlockSpec(memory_space=pltpu.VMEM)
HBM = pl.BlockSpec(memory_space=pltpu.HBM)


def in_hbm(x):
    return pltpu.with_memory_space_constraint(x, pltpu.HBM)


def in_vmem(x):
    return pltpu.with_memory_space_constraint(x, pltpu.VMEM)


def dot(a, b):
    return jnp.dot(a, b, preferred_element_type=F32)


def group_at(g, d):
    return g + (d % 2) * jnp.where(lax.rem(g, 2) == 0, 1, -1) + (d // 2) * jnp.where(g < 2, 2, -2)


def iota(shape, axis):
    return lax.broadcasted_iota(jnp.int32, shape, axis)


def build_table(my_sub, cols, slots, table):
    slot = jnp.concatenate([slots[p, :, q, :] for p in range(SLOTS_P) for q in range(SLOTS_P)], axis=1)
    bucket_of = (slot >> 5) * WIN + ((slot & (N_SUB - 1)) - my_sub + 2)
    col = jnp.concatenate([cols[...]] * 4, axis=1)
    rows = SLOTS_A
    one_hot = [
        (jnp.broadcast_to(bucket_of[r : r + 1, :], (WIDTH, B)) == iota((WIDTH, B), 0)).astype(F32) for r in range(rows)
    ]
    stacked = jnp.concatenate(one_hot, axis=0).astype(BF)
    upper = (iota((B, B), 0) < iota((B, B), 1)).astype(F32).astype(BF)
    rank = dot(stacked, upper)
    total = dot(stacked, jnp.ones((B, B), BF))
    base = jnp.zeros((WIDTH, B), F32)
    ranks = []
    for r in range(rows):
        ranks.append(base + rank[r * WIDTH : (r + 1) * WIDTH])
        base = base + total[r * WIDTH : (r + 1) * WIDTH]
    bucket = iota((WIDTH, B), 0)
    used = ((base.astype(jnp.int32) + (U - 1)) >> (U.bit_length() - 1)).astype(F32)
    used = jnp.where(bucket < BUCKETS, jnp.maximum(used, 1.0), 0.0)
    lower = (iota((WIDTH, WIDTH), 1) < iota((WIDTH, WIDTH), 0)).astype(F32)
    first = jnp.dot(lower, used, precision=lax.Precision.HIGHEST, preferred_element_type=F32)
    lane = iota((1, B), 1)
    i = lane & (ROWS - 1)
    p = lane >> 6
    q = (lane >> 5) & 1
    words = jnp.zeros((3 * WORD_ROWS, B), F32)
    for r in range(rows):
        pos = jnp.sum(one_hot[r] * (first * float(U) + ranks[r]), axis=0, keepdims=True).astype(jnp.int32)
        left = (i * SLOTS_A + r) * 2 + p + 2
        here = jnp.broadcast_to(pos >> 7, (WORD_ROWS, B)) == iota((WORD_ROWS, B), 0)
        parts = [
            jnp.where(here, jnp.broadcast_to(v.astype(F32), (WORD_ROWS, B)), 0.0)
            for v in (col[r : r + 1, :] * 2 + q, left >> 4, left & 15)
        ]
        low = (jnp.broadcast_to(pos & (B - 1), (B, B)) == iota((B, B), 0)).astype(F32).astype(BF)
        words = words + lax.dot_general(
            jnp.concatenate(parts, axis=0).astype(BF),
            low,
            (((1,), (1,)), ((), ())),
            preferred_element_type=F32,
        )
    words = words.astype(jnp.int32)
    table[0:WORD_ROWS, :] = words[:WORD_ROWS] * 1024 + words[WORD_ROWS : 2 * WORD_ROWS] * 16 + words[2 * WORD_ROWS :]
    starts = jnp.where(bucket < BUCKETS, first, -1.0)
    chunk = iota((WIDTH, B), 1).astype(F32)
    keep = [
        1.0 - jnp.sum((starts == chunk + float(h * B)).astype(F32), axis=0, keepdims=True) for h in range(KEEP_ROWS)
    ]
    last = jnp.sum(jnp.where(bucket == iota((WIDTH, B), 1), first + used - 1.0, 0.0), axis=0, keepdims=True)
    rest = jnp.concatenate(keep + [last, jnp.zeros((7 - KEEP_ROWS, B), F32)], axis=0)
    table[WORD_ROWS:TABLE_ROWS, :] = rest.astype(jnp.int32)


def left_kernel(
    cols_hbm, slots_hbm, send_hbm, a_hbm, p_hbm, lefts, rights, table,
    cols, slots, halo_send, a_v, p_v, packed, a_sems, p_sems, send_sems, recv_sems,
):
    g = lax.axis_index("group")
    s = lax.axis_index("sub")
    sides = ((s > 0, (g, jnp.maximum(s - 1, 0))), (s < N_SUB - 1, (g, jnp.minimum(s + 1, N_SUB - 1))))
    barrier = pltpu.get_barrier_semaphore()
    for there, peer in sides:

        @pl.when(there)
        def _():
            pl.semaphore_signal(barrier, inc=1, device_id=peer, device_id_type=MESH)

    load = pltpu.make_async_copy(p_hbm, p_v, p_sems.at[0])
    keep = pltpu.make_async_copy(p_hbm, rights.at[pl.ds(0, OWN_BLOCKS)], p_sems.at[1])
    small = [
        pltpu.make_async_copy(src, dst, p_sems.at[2 + n])
        for n, (src, dst) in enumerate(((send_hbm, halo_send), (cols_hbm, cols), (slots_hbm, slots)))
    ]
    small[0].start()
    load.start()
    small[1].start()
    small[2].start()

    def fetch(i):
        place = lax.rem(i, ROW_RING)
        return pltpu.make_async_copy(a_hbm.at[i], a_v.at[place], a_sems.at[place])

    for i in range(ROW_RING):
        fetch(i).start()
    keep.start()
    for copy in small:
        copy.wait()
    zero = jnp.zeros((B, B), BF)
    load.wait()
    for j in range(2 * HALO):
        row = halo_send[j]
        for q in range(SLOTS_P):
            packed[j * 2 + q] = p_v[row * 2 + q]
    half = FAR_BLOCKS // 2
    copies = []
    for n, (there, peer) in enumerate(sides):
        copies.append(
            pltpu.make_async_remote_copy(
                src_ref=packed.at[pl.ds(n * half, half)],
                dst_ref=rights.at[pl.ds(OWN_BLOCKS + half - n * half, half)],
                send_sem=send_sems.at[n],
                recv_sem=recv_sems.at[n],
                device_id=peer,
                device_id_type=MESH,
            )
        )
    pl.semaphore_wait(barrier, sum(there.astype(jnp.int32) for there, _ in sides))
    for (there, _), copy in zip(sides, copies):

        @pl.when(there)
        def _():
            copy.start()

    lefts[0] = zero
    lefts[1] = zero
    build_table(s, cols, slots, table)

    @pl.loop(0, ROWS // ROW_STEP)
    def _(step):
        for r in range(ROW_STEP):
            fetch(step * ROW_STEP + r).wait()
        for r in range(ROW_STEP):
            i = step * ROW_STEP + r
            place = lax.rem(i, ROW_RING)
            p_t = jnp.concatenate([p_v[i * 2].T, p_v[i * 2 + 1].T], axis=0)
            first = i * (2 * SLOTS_A) + 2
            for k in range(0, SLOTS_A - 1, 2):
                y = dot(p_t, jnp.concatenate([a_v[place, k], a_v[place, k + 1]], axis=1)).astype(BF)
                for n in range(2):
                    for p in range(SLOTS_P):
                        lefts[first + (k + n) * 2 + p] = y[p * B : (p + 1) * B, n * B : (n + 1) * B]
            k = SLOTS_A - 1
            both = jnp.concatenate([p_t[:B], p_t[B:]], axis=1)
            top = jnp.concatenate([a_v[place, k], zero], axis=1)
            bottom = jnp.concatenate([zero, a_v[place, k]], axis=1)
            y = dot(both, jnp.concatenate([top, bottom], axis=0)).astype(BF)
            for p in range(SLOTS_P):
                lefts[first + k * 2 + p] = y[:, p * B : (p + 1) * B]
        for r in range(ROW_STEP):
            i = step * ROW_STEP + r + ROW_RING

            @pl.when(i < ROWS)
            def _():
                fetch(i).start()

    keep.wait()
    for n, (there, _) in enumerate(sides):

        @pl.when(there)
        def _():
            copies[n].wait_send()
            copies[1 - n].wait_recv()

        @pl.when(jnp.logical_not(there))
        def _():
            rights[pl.ds(OWN_BLOCKS + n * half, half)] = jnp.zeros((half, B, B), BF)


def left_blocks(cols, slots, halo_send, a_vals, p_blocks):
    return pl.pallas_call(
        left_kernel,
        out_shape=(
            pltpu.VMEM((LEFTS, B, B), BF),
            pltpu.VMEM((OWN_BLOCKS + FAR_BLOCKS, B, B), BF),
            jax.ShapeDtypeStruct((TABLE_ROWS, B), jnp.int32),
        ),
        in_specs=[HBM] * 5,
        out_specs=(VMEM, VMEM, VMEM),
        scratch_shapes=[
            pltpu.VMEM((SLOTS_A, ROWS), jnp.int32),
            pltpu.VMEM((SLOTS_P, SLOTS_A, SLOTS_P, ROWS), jnp.int32),
            pltpu.SMEM((2 * HALO,), jnp.int32),
            pltpu.VMEM((ROW_RING, SLOTS_A, B, B), BF),
            pltpu.VMEM((OWN_BLOCKS, B, B), BF),
            pltpu.VMEM((FAR_BLOCKS, B, B), BF),
            pltpu.SemaphoreType.DMA((ROW_RING,)),
            pltpu.SemaphoreType.DMA((5,)),
            pltpu.SemaphoreType.DMA((2,)),
            pltpu.SemaphoreType.DMA((2,)),
        ],
        compiler_params=pltpu.CompilerParams(collective_id=0, has_side_effects=True, vmem_limit_bytes=10 * MIB),
        name="left_blocks",
    )(*[in_hbm(x) for x in (cols, slots, halo_send, a_vals, p_blocks)])


def term_kernel(table, lefts, rights, received, scales, run, coded, scale, sems):
    g = lax.axis_index("group")
    s = lax.axis_index("sub")
    peers = []
    for off in (2, -2, 1, -1, 0):
        for dg in (3, 2, 1, 0):
            if dg or off:
                there = jnp.logical_and(s + off >= 0, s + off < N_SUB)
                ts = jnp.clip(s + off, 0, N_SUB - 1)
                tg = group_at(g, dg)
                peers.append((dg, off, there, tg, ts))
    barrier = pltpu.get_barrier_semaphore()
    for _, _, there, tg, ts in peers:

        @pl.when(there)
        def _():
            pl.semaphore_signal(barrier, inc=1, device_id=(tg, ts), device_id_type=MESH)

    def step(it, acc):
        for n in range(G):
            c = it * G + n
            left, right = [], []
            for u in range(U):
                w = table[c * U + u]
                left.append(lefts[w & 1023])
                right.append(rights[w >> 10])
            keep = table[WORD_ROWS * B + c].astype(F32)
            acc = acc * keep + dot(jnp.concatenate(left, axis=1), jnp.concatenate(right, axis=0))
            run[c] = acc
        return acc

    lax.fori_loop(0, CHUNKS // G, step, jnp.zeros((B, B), F32))

    def code(bucket):
        total = run[table[(WORD_ROWS + KEEP_ROWS) * B + bucket]]
        top = jnp.maximum(jnp.max(jnp.abs(total), axis=0, keepdims=True), 1e-30)
        return jnp.round(total * (CODE / top)).astype(jnp.int32).astype(I16), top * (1.0 / CODE)

    pl.semaphore_wait(barrier, sum(peer[2].astype(jnp.int32) for peer in peers))

    copies = []
    for dg, off, there, tg, ts in peers:
        j = dg * WIN + off + 2
        pair = [
            pltpu.make_async_remote_copy(
                src_ref=src.at[j],
                dst_ref=dst.at[j],
                send_sem=sems.at[2 * n, j],
                recv_sem=sems.at[2 * n + 1, j],
                device_id=(tg, ts),
                device_id_type=MESH,
            )
            for n, (src, dst) in enumerate(((coded, received), (scale, scales)))
        ]
        copies.append(pair)

        @pl.when(there)
        def _():
            coded[j], scale[j] = code(tg * WIN + (off + 2))
            for copy in pair:
                copy.start()

    received[2], scales[2] = code(g * WIN + 2)
    for (dg, off, there, _, _), pair in zip(peers, copies):
        from_there = jnp.logical_and(s - off >= 0, s - off < N_SUB)

        @pl.when(there)
        def _():
            for copy in pair:
                copy.wait_send()

        @pl.when(from_there)
        def _():
            for copy in pair:
                copy.wait_recv()


def send_terms(table, lefts, rights):
    return pl.pallas_call(
        term_kernel,
        out_shape=(pltpu.VMEM((BUCKETS, B, B), I16), pltpu.VMEM((BUCKETS, 1, B), F32)),
        in_specs=[SMEM, VMEM, VMEM],
        out_specs=(VMEM, VMEM),
        scratch_shapes=[
            pltpu.VMEM((CHUNKS, B, B), F32),
            pltpu.VMEM((BUCKETS, B, B), I16),
            pltpu.VMEM((BUCKETS, 1, B), F32),
            pltpu.SemaphoreType.DMA((4, BUCKETS)),
        ],
        compiler_params=pltpu.CompilerParams(collective_id=1, has_side_effects=True, vmem_limit_bytes=22 * MIB),
        name="send_terms",
    )(table, in_vmem(lefts), in_vmem(rights))


def place_kernel(targets_hbm, received, scales, out_hbm, targets, out, sems):
    g = lax.axis_index("group")
    s = lax.axis_index("sub")
    load = pltpu.make_async_copy(targets_hbm, targets, sems.at[0])
    load.start()
    out[...] = jnp.zeros_like(out)
    load.wait()
    for dg in range(N_GROUP):
        sg = group_at(g, dg)
        for off in range(-2, 3):
            j = dg * WIN + off + 2
            ss = s - off
            inside = jnp.logical_and(ss >= 0, ss < N_SUB)
            o = jnp.where(inside, targets[sg * N_SUB + jnp.clip(ss, 0, N_SUB - 1)], OWN)
            block = received[j].astype(jnp.int32).astype(F32) * scales[j]
            out[o] += jnp.where(inside, block, 0.0)
    save = pltpu.make_async_copy(out.at[pl.ds(0, OWN)], out_hbm, sems.at[1])
    save.start()
    save.wait()


def place(targets, received, scales):
    return pl.pallas_call(
        place_kernel,
        out_shape=jax.ShapeDtypeStruct((OWN, B, B), F32),
        in_specs=[HBM, VMEM, VMEM],
        out_specs=HBM,
        scratch_shapes=[
            pltpu.SMEM((N_GROUP * N_SUB,), jnp.int32),
            pltpu.VMEM((OWN + 1, B, B), F32),
            pltpu.SemaphoreType.DMA((2,)),
        ],
        name="place",
    )(in_hbm(targets), in_vmem(received), in_vmem(scales))


def per_device(a_vals, a_cols, p_vals, halo_send, send_slot, recv_block):
    lefts, rights, table = left_blocks(
        a_cols.T, send_slot.transpose(1, 2, 3, 0), halo_send, a_vals, p_vals.reshape(OWN_BLOCKS, B, B)
    )
    received, scales = send_terms(table.reshape(-1), lefts, rights)
    return place(recv_block, received, scales)


def solution(mesh):
    return jax.shard_map(
        per_device,
        mesh=mesh,
        in_specs=(
            P(("group", "sub"), None, None, None),
            P(("group", "sub"), None),
            P(("group", "sub"), None, None, None),
            P(("group", "sub")),
            P(("group", "sub"), None, None, None),
            P(("group", "sub")),
        ),
        out_specs=P(("group", "sub"), None, None),
        check_vma=False,
    )
```

time: 409 us -> 38.5 us (0.09)
  matrix products: 170 us -> 0 us
  local copies, waits for them, and re-layouts: 109 us -> 0 us
  blocking collectives: 108 us -> 0 us
  Pallas kernels: 0 us -> 38.4 us
  starting transfers between devices: 7.67 us -> 0 us
  waiting for transfers between devices: 5.77 us -> 0 us
    dot_general x14 -> x0, matrix products: 170 us -> none  [the longest x5 103 us: gather_sum(): jnp.dot(picker, values.reshape(values.shape[0], -1), precision=lax.Precis...]
    all_to_all x1 -> x0, blocking collectives: 108 us -> none  [per_device(): lax.all_to_all(flat_sums, ('group', 'sub'), split_axis=0, concat_axis=0,...]
    transpose x4 -> x0, local copies, waits for them, and re-layouts: 74.9 us -> none  [advance(): jnp.einsum('rpux,rkquy->rpkqxy', own_block, product, preferred_element_ty...]
    pallas_call x0 -> x3, Pallas kernels: none -> 38.4 us  [the longest x1 22.7 us: send_terms(): pl.pallas_call(term_kernel, out_shape=(pltpu.VMEM((BUCKETS, B, B), I16),...]
    while x5 -> x0, local copies, waits for them, and re-layouts: 15.6 us -> none
    all_to_all x1 -> x0, local copies, waits for them, and re-layouts: 9.31 us -> none  [per_device(): lax.all_to_all(flat_sums, ('group', 'sub'), split_axis=0, concat_axis=0,...]
    ppermute x2 -> x0, starting transfers between devices: 7.67 us -> none  [the longest x1 5.75 us: with_halo(): after = lax.ppermute(initial, axis, down)]
    ppermute x2 -> x0, waiting for transfers between devices: 5.77 us -> none  [the longest x1 4.71 us: with_halo(): before = lax.ppermute(last, axis, up)]
  transfers between devices with their start and end apart: 2 -> 0, of which waited for: 2 -> 0; matrix products, arithmetic and copies ran while one was open for 0% -> 0% of each run, Pallas kernels for 0% -> 0%
where the time goes in v3:
time: 38.5 us; the launch traced here: 38.4 us
  Pallas kernels  38.4 us (100%)
    pallas_call x1, Pallas kernels, send_terms(): pl.pallas_call(term_kernel, out_shape=(pltpu.VMEM((BUCKETS, B, B), I16),...  22.7 us
    pallas_call x1, Pallas kernels, left_blocks(): pl.pallas_call(left_kernel, out_shape=(pltpu.VMEM((LEFTS, B, B), BF), plt...  13.5 us
    pallas_call x1, Pallas kernels, place(): pl.pallas_call(place_kernel, out_shape=jax.ShapeDtypeStruct((OWN, B, B),...  2.22 us

profile of v3, /device:TPU:24, one launch (start us, length us, event | category | flops | bytes accessed | tf_op | source)
XLA Modules:
  0.0 38.4 jit_solution(17291869246497551615)
XLA Ops:
  0.0 13.5 %left_blocks.1 = (bf16[584,128,128]{2,1,0:T(8,128)(2,1)S(1)}, bf16[96,128,128]{2,1,0:T(8,128)(2,1)S(1)}, s32[24,128]{1,0:T(8,128)S(1)}) custom-call(s32[9,32]{1,0:T(8,128)} %bitcast.7, s32[2,9,2,32]{3,2,1,0:T(2,128)} %bitcast.6, s32[16]{0:T(128)} %send_hbm.1, bf16[32,9,128,128]{3,2,1,0:T(8,128)(2,1)} %a_hbm.1, bf16[64,128,128]{2,1,0:T(8,128)(2,1)} %bitcast.5), custom_call_target="tpu_custom_call" | custom-call | tf_op jit(solution)/shard_map/left_blocks/pallas_call | solution.py:225
  13.5 22.7 %send_terms.1 = (s16[20,128,128]{2,1,0:T(8,128)(2,1)S(1)}, f32[20,1,128]{2,1,0:T(1,128)S(1)}) custom-call(s32[3072]{0:T(1024)S(1)} %bitcast.4, bf16[584,128,128]{2,1,0:T(8,128)(2,1)S(1)} %get-tuple-element.11.lefts, bf16[96,128,128]{2,1,0:T(8,128)(2,1)S(1)} %get-tuple-element.12.rights), custom_call_target="tpu_custom_call" | custom-call | tf_op jit(solution)/shard_map/send_terms/pallas_call | solution.py:329
  36.2 2.2 %place.1 = f32[32,128,128]{2,1,0:T(8,128)} custom-call(s32[128]{0:T(128)} %targets_hbm.1, s16[20,128,128]{2,1,0:T(8,128)(2,1)S(1)} %get-tuple-element.13.received, f32[20,1,128]{2,1,0:T(1,128)S(1)} %get-tuple-element.14.scales), custom_call_target="tpu_custom_call" | custom-call | tf_op jit(solution)/shard_map/place/pallas_call | solution.py:367

commit v4 on v3

v4 whole, which is shorter than its diff:
```python
import functools

import jax
import jax.numpy as jnp
from jax import lax
from jax.experimental import pallas as pl
from jax.experimental.pallas import tpu as pltpu
from jax.sharding import PartitionSpec as P

B = 128
ROWS = 32
SLOTS_A = 9
SLOTS_P = 2
HALO = 8
OWN = 32
N_GROUP = 4
N_SUB = 32
ENTRIES = ROWS * SLOTS_A
TERMS = ENTRIES * 4
WIN = 5
BUCKETS = N_GROUP * WIN
ROW_STEP = 4
ROW_RING = 16
U = 4
G = 154
STEPS = 2
STEP_ROWS = 5
KEEP_ROWS = 2
LEFTS = 2 * ENTRIES + 8
OWN_BLOCKS = ROWS * SLOTS_P
FAR_BLOCKS = 2 * HALO * SLOTS_P
RIGHTS = 128
WIDTH = 32
WORD_ROWS = 16
LAST_ROW = WORD_ROWS + STEPS * KEEP_ROWS
FROM_ROW = LAST_ROW + 1
TABLE_ROWS = 24
CODE = 32767.0
MIB = 2**20
LIMIT = 54
MESH = pl.DeviceIdType.MESH
BF = jnp.bfloat16
F32 = jnp.float32
I16 = jnp.int16
SMEM = pl.BlockSpec(memory_space=pltpu.SMEM)
VMEM = pl.BlockSpec(memory_space=pltpu.VMEM)
HBM = pl.BlockSpec(memory_space=pltpu.HBM)


def in_hbm(x):
    return pltpu.with_memory_space_constraint(x, pltpu.HBM)


def in_vmem(x):
    return pltpu.with_memory_space_constraint(x, pltpu.VMEM)


def dot(a, b):
    return jnp.dot(a, b, preferred_element_type=F32)


def group_at(g, d):
    return g + (d % 2) * jnp.where(lax.rem(g, 2) == 0, 1, -1) + (d // 2) * jnp.where(g < 2, 2, -2)


def iota(shape, axis):
    return lax.broadcasted_iota(jnp.int32, shape, axis)


def build_table(g, my_sub, cols, slots, targets, table):
    slot = jnp.concatenate([slots[p, :, q, :] for p in range(SLOTS_P) for q in range(SLOTS_P)], axis=1)
    bucket_of = (slot >> 5) * WIN + ((slot & (N_SUB - 1)) - my_sub + 2)
    known = jnp.logical_and(bucket_of >= 0, bucket_of < BUCKETS)
    col = jnp.concatenate([cols[...]] * 4, axis=1)
    rows = SLOTS_A
    one_hot = [
        (jnp.broadcast_to(bucket_of[r : r + 1, :], (WIDTH, B)) == iota((WIDTH, B), 0)).astype(F32) for r in range(rows)
    ]
    stacked = jnp.concatenate(one_hot, axis=0).astype(BF)
    upper = (iota((B, B), 0) < iota((B, B), 1)).astype(F32).astype(BF)
    rank = dot(stacked, upper)
    total = dot(stacked, jnp.ones((B, B), BF))
    base = jnp.zeros((WIDTH, B), F32)
    ranks = []
    for r in range(rows):
        ranks.append(base + rank[r * WIDTH : (r + 1) * WIDTH])
        base = base + total[r * WIDTH : (r + 1) * WIDTH]
    bucket = iota((WIDTH, B), 0)
    used = ((base.astype(jnp.int32) + (U - 1)) >> (U.bit_length() - 1)).astype(F32)
    used = jnp.where(bucket < BUCKETS, jnp.maximum(used, 1.0), 0.0)
    lower = (iota((WIDTH, WIDTH), 1) < iota((WIDTH, WIDTH), 0)).astype(F32)
    first = jnp.dot(lower, used, precision=lax.Precision.HIGHEST, preferred_element_type=F32)
    lane = iota((1, B), 1)
    i = lane & (ROWS - 1)
    p = lane >> 6
    q = (lane >> 5) & 1
    words = jnp.zeros((3 * WORD_ROWS, B), F32)
    for r in range(rows):
        pos = jnp.sum(one_hot[r] * (first * float(U) + ranks[r]), axis=0, keepdims=True).astype(jnp.int32)
        pos = jnp.where(known[r : r + 1, :], pos, -1)
        step = sum((pos >= n * G * U).astype(jnp.int32) for n in range(1, STEPS))
        pos = pos + step * (STEP_ROWS * B - G * U)
        left = (i * SLOTS_A + r) * 2 + p + 2
        here = jnp.broadcast_to(pos >> 7, (WORD_ROWS, B)) == iota((WORD_ROWS, B), 0)
        parts = [
            jnp.where(here, jnp.broadcast_to(v.astype(F32), (WORD_ROWS, B)), 0.0)
            for v in (col[r : r + 1, :] * 2 + q, left >> 4, left & 15)
        ]
        low = (jnp.broadcast_to(pos & (B - 1), (B, B)) == iota((B, B), 0)).astype(F32).astype(BF)
        words = words + lax.dot_general(
            jnp.concatenate(parts, axis=0).astype(BF),
            low,
            (((1,), (1,)), ((), ())),
            preferred_element_type=F32,
        )
    words = words.astype(jnp.int32)
    table[0:WORD_ROWS, :] = words[:WORD_ROWS] * 1024 + words[WORD_ROWS : 2 * WORD_ROWS] * 16 + words[2 * WORD_ROWS :]
    starts = jnp.where(bucket < BUCKETS, first, -1.0)
    chunk = iota((WIDTH, B), 1).astype(F32)
    keep = [
        1.0 - jnp.sum((starts == chunk + float(n * G + h * B)).astype(F32), axis=0, keepdims=True)
        for n in range(STEPS)
        for h in range(KEEP_ROWS)
    ]
    last = jnp.sum(jnp.where(bucket == iota((WIDTH, B), 1), first + used - 1.0, 0.0), axis=0, keepdims=True)
    away = (lane & (N_SUB - 1)) - my_sub
    near = jnp.logical_and(away >= -2, away <= 2)
    slot = ((lane >> 5) ^ g) * WIN + 2 - away
    owned = jnp.where(near, targets[...], OWN)
    takes = (jnp.broadcast_to(owned, (WIDTH, B)) == bucket).astype(F32)
    order = dot(takes.astype(BF), upper)
    count = dot(takes.astype(BF), jnp.ones((B, B), BF))
    start = dot(lower.astype(BF), count.astype(BF))
    pos = jnp.sum(takes * (start + order), axis=0, keepdims=True).astype(jnp.int32)
    pos = jnp.where(jnp.logical_and(near, owned < OWN), pos, -1)
    spread = (jnp.broadcast_to(pos, (B, B)) == iota((B, B), 0)).astype(F32).astype(BF)
    source = lax.dot_general(
        jnp.broadcast_to(slot.astype(F32), (8, B)).astype(BF),
        spread,
        (((1,), (1,)), ((), ())),
        preferred_element_type=F32,
    )[0:1]
    opens = jnp.where(count > 0.0, start, -1.0)
    join = 1.0 - jnp.sum((opens == chunk).astype(F32), axis=0, keepdims=True)
    final = jnp.where(count > 0.0, start + count - 1.0, float(BUCKETS))
    final = jnp.sum(jnp.where(bucket == iota((WIDTH, B), 1), final, 0.0), axis=0, keepdims=True)
    rest = jnp.concatenate(keep + [last, source, join, final], axis=0)
    table[WORD_ROWS:TABLE_ROWS, :] = rest.astype(jnp.int32)


def terms_kernel(
    cols_hbm, slots_hbm, send_hbm, targets_hbm, a_hbm, p_hbm, out,
    cols, slots, halo_send, targets, a_v, p_v, packed, lefts, rights, table_v, table, run, coded, scale, received, scales,
    a_sems, in_sems, send_sems, recv_sems, sems,
):
    g = lax.axis_index("group")
    s = lax.axis_index("sub")
    sides = ((s > 0, (g, jnp.maximum(s - 1, 0))), (s < N_SUB - 1, (g, jnp.minimum(s + 1, N_SUB - 1))))
    peers = []
    for off in (2, -2, 1, -1, 0):
        for dg in (3, 2, 1, 0):
            if dg or off:
                there = jnp.logical_and(s + off >= 0, s + off < N_SUB)
                ts = jnp.clip(s + off, 0, N_SUB - 1)
                peers.append((dg, off, there, group_at(g, dg), ts))
    load = pltpu.make_async_copy(p_hbm, p_v, in_sems.at[0])
    small = [
        pltpu.make_async_copy(src, dst, in_sems.at[1 + n])
        for n, (src, dst) in enumerate(((send_hbm, halo_send), (cols_hbm, cols), (slots_hbm, slots), (targets_hbm, targets)))
    ]
    small[0].start()
    load.start()
    small[1].start()
    small[2].start()
    small[3].start()
    barrier = pltpu.get_barrier_semaphore()
    for _, _, there, tg, ts in peers:

        @pl.when(there)
        def _():
            pl.semaphore_signal(barrier, inc=1, device_id=(tg, ts), device_id_type=MESH)

    def fetch(i):
        place = lax.rem(i, ROW_RING)
        return pltpu.make_async_copy(a_hbm.at[i], a_v.at[place], a_sems.at[place])

    for i in range(ROW_RING):
        fetch(i).start()
    for copy in small:
        copy.wait()
    zero = jnp.zeros((B, B), BF)
    load.wait()
    for j in range(2 * HALO):
        row = halo_send[j]
        for q in range(SLOTS_P):
            packed[j * 2 + q] = p_v[(row & (ROWS - 1)) * 2 + q]
    half = FAR_BLOCKS // 2
    copies = []
    for n, (there, peer) in enumerate(sides):
        copies.append(
            pltpu.make_async_remote_copy(
                src_ref=packed.at[pl.ds(n * half, half)],
                dst_ref=rights.at[pl.ds(OWN_BLOCKS + half - n * half, half)],
                send_sem=send_sems.at[n],
                recv_sem=recv_sems.at[n],
                device_id=peer,
                device_id_type=MESH,
            )
        )
    pl.semaphore_wait(barrier, sum(peer[2].astype(jnp.int32) for peer in peers))
    for (there, _), copy in zip(sides, copies):

        @pl.when(there)
        def _():
            copy.start()

    lefts[0] = zero
    lefts[1] = zero
    build_table(g, s, cols, slots, targets, table_v)
    move = pltpu.make_async_copy(table_v, table, in_sems.at[5])
    move.start()

    @pl.loop(0, ROWS // ROW_STEP)
    def _(step):
        for r in range(ROW_STEP):
            fetch(step * ROW_STEP + r).wait()
        for r in range(ROW_STEP):
            i = step * ROW_STEP + r
            place = lax.rem(i, ROW_RING)
            p_t = jnp.concatenate([p_v[i * 2].T, p_v[i * 2 + 1].T], axis=0)
            for p in range(SLOTS_P):
                rights[i * 2 + p] = p_v[i * 2 + p]
            first = i * (2 * SLOTS_A) + 2
            for k in range(0, SLOTS_A - 1, 2):
                y = dot(p_t, jnp.concatenate([a_v[place, k], a_v[place, k + 1]], axis=1)).astype(BF)
                for n in range(2):
                    for p in range(SLOTS_P):
                        lefts[first + (k + n) * 2 + p] = y[p * B : (p + 1) * B, n * B : (n + 1) * B]
            k = SLOTS_A - 1
            both = jnp.concatenate([p_t[:B], p_t[B:]], axis=1)
            top = jnp.concatenate([a_v[place, k], zero], axis=1)
            bottom = jnp.concatenate([zero, a_v[place, k]], axis=1)
            y = dot(both, jnp.concatenate([top, bottom], axis=0)).astype(BF)
            for p in range(SLOTS_P):
                lefts[first + k * 2 + p] = y[:, p * B : (p + 1) * B]
        for r in range(ROW_STEP):
            i = step * ROW_STEP + r + ROW_RING

            @pl.when(i < ROWS)
            def _():
                fetch(i).start()

    move.wait()
    for n, (there, _) in enumerate(sides):

        @pl.when(there)
        def _():
            copies[n].wait_send()
            copies[1 - n].wait_recv()

        @pl.when(jnp.logical_not(there))
        def _():
            rights[pl.ds(OWN_BLOCKS + n * half, half)] = jnp.zeros((half, B, B), BF)

    def step(it, acc):
        for n in range(G):
            left, right = [], []
            for u in range(n * U, n * U + U):
                w = table[it * STEP_ROWS + u // B, u % B]
                left.append(lefts[jnp.minimum(w & 1023, LEFTS - 1)])
                right.append(rights[(w >> 10) & (RIGHTS - 1)])
            keep = table[WORD_ROWS + it * KEEP_ROWS + n // B, n % B].astype(F32)
            acc = acc * keep + dot(jnp.concatenate(left, axis=1), jnp.concatenate(right, axis=0))
            run[it * G + n] = acc
        return acc

    lax.fori_loop(0, STEPS, step, jnp.zeros((B, B), F32))

    def code(bucket):
        total = run[jnp.clip(table[LAST_ROW, bucket], 0, STEPS * G - 1)]
        top = jnp.maximum(jnp.max(jnp.abs(total), axis=0, keepdims=True), 1e-30)
        return jnp.round(total * (CODE / top)).astype(jnp.int32).astype(I16), top * (1.0 / CODE)


    copies = []
    for dg, off, there, tg, ts in peers:
        j = dg * WIN + off + 2
        pair = [
            pltpu.make_async_remote_copy(
                src_ref=src.at[j],
                dst_ref=dst.at[j],
                send_sem=sems.at[2 * n, j],
                recv_sem=sems.at[2 * n + 1, j],
                device_id=(tg, ts),
                device_id_type=MESH,
            )
            for n, (src, dst) in enumerate(((coded, received), (scale, scales)))
        ]
        copies.append(pair)

        @pl.when(there)
        def _():
            coded[j], scale[j] = code(tg * WIN + (off + 2))
            for copy in pair:
                copy.start()

    received[2], scales[2] = code(g * WIN + 2)
    for (dg, off, there, _, _), pair in zip(peers, copies):
        from_there = jnp.logical_and(s - off >= 0, s - off < N_SUB)

        @pl.when(there)
        def _():
            for copy in pair:
                copy.wait_send()

        @pl.when(from_there)
        def _():
            for copy in pair:
                copy.wait_recv()

    acc = jnp.zeros((B, B), F32)
    run[BUCKETS] = acc
    for n in range(BUCKETS):
        j = jnp.clip(table[FROM_ROW, n], 0, BUCKETS - 1)
        acc = acc * table[FROM_ROW + 1, n].astype(F32) + received[j].astype(jnp.int32).astype(F32) * scales[j]
        run[n] = acc
    for o in range(OWN):
        out[o] = run[jnp.clip(table[FROM_ROW + 2, o], 0, BUCKETS)]


def sum_terms(cols, slots, halo_send, targets, a_vals, p_blocks):
    return pl.pallas_call(
        terms_kernel,
        out_shape=pltpu.VMEM((OWN, B, B), F32),
        in_specs=[HBM] * 6,
        out_specs=VMEM,
        scratch_shapes=[
            pltpu.VMEM((SLOTS_A, ROWS), jnp.int32),
            pltpu.VMEM((SLOTS_P, SLOTS_A, SLOTS_P, ROWS), jnp.int32),
            pltpu.SMEM((2 * HALO,), jnp.int32),
            pltpu.VMEM((1, N_GROUP * N_SUB), jnp.int32),
            pltpu.VMEM((ROW_RING, SLOTS_A, B, B), BF),
            pltpu.VMEM((OWN_BLOCKS, B, B), BF),
            pltpu.VMEM((FAR_BLOCKS, B, B), BF),
            pltpu.VMEM((LEFTS, B, B), BF),
            pltpu.VMEM((RIGHTS, B, B), BF),
            pltpu.VMEM((TABLE_ROWS, B), jnp.int32),
            pltpu.SMEM((TABLE_ROWS, B), jnp.int32),
            pltpu.VMEM((STEPS * G, B, B), F32),
            pltpu.VMEM((BUCKETS, B, B), I16),
            pltpu.VMEM((BUCKETS, 1, B), F32),
            pltpu.VMEM((BUCKETS, B, B), I16),
            pltpu.VMEM((BUCKETS, 1, B), F32),
            pltpu.SemaphoreType.DMA((ROW_RING,)),
            pltpu.SemaphoreType.DMA((6,)),
            pltpu.SemaphoreType.DMA((2,)),
            pltpu.SemaphoreType.DMA((2,)),
            pltpu.SemaphoreType.DMA((4, BUCKETS)),
        ],
        compiler_params=pltpu.CompilerParams(collective_id=0, has_side_effects=True, vmem_limit_bytes=LIMIT * MIB),
        name="sum_terms",
    )(*[in_hbm(x) for x in (cols, slots, halo_send, targets, a_vals, p_blocks)])


def per_device(a_vals, a_cols, p_vals, halo_send, send_slot, recv_block):
    slots = send_slot.transpose(1, 2, 3, 0)
    targets = recv_block.reshape(1, -1)
    return sum_terms(a_cols.T, slots, halo_send, targets, a_vals, p_vals.reshape(OWN_BLOCKS, B, B))


def solution(mesh):
    return jax.shard_map(
        per_device,
        mesh=mesh,
        in_specs=(
            P(("group", "sub"), None, None, None),
            P(("group", "sub"), None),
            P(("group", "sub"), None, None, None),
            P(("group", "sub")),
            P(("group", "sub"), None, None, None),
            P(("group", "sub")),
        ),
        out_specs=P(("group", "sub"), None, None),
        check_vma=False,
    )
```

time: 38.5 us -> 37.1 us (0.964)
  Pallas kernels: 38.4 us -> 35.6 us
  local copies, waits for them, and re-layouts: 0 us -> 1.32 us
    pallas_call x3 -> x1, Pallas kernels: 38.4 us -> 35.6 us  [sum_terms(): pl.pallas_call(terms_kernel, out_shape=pltpu.VMEM((OWN, B, B), F32), in_s...]
    unnamed x0 -> x1, local copies, waits for them, and re-layouts: none -> 1.32 us
where the time goes in v4:
time: 37.1 us; the launch traced here: 37 us
  Pallas kernels  35.6 us (96%)
  local copies, waits for them, and re-layouts  1.32 us (4%)
    pallas_call x1, Pallas kernels, sum_terms(): pl.pallas_call(terms_kernel, out_shape=pltpu.VMEM((OWN, B, B), F32), in_s...  35.6 us
    unnamed x1, local copies, waits for them, and re-layouts  1.32 us

profile of v4, /device:TPU:24, one launch (start us, length us, event | category | flops | bytes accessed | tf_op | source)
XLA Modules:
  0.0 37.0 jit_solution(4418873708605362151)
XLA Ops:
  0.0 35.6 %sum_terms.1 = f32[32,128,128]{2,1,0:T(8,128)S(1)} custom-call(s32[9,32]{1,0:T(8,128)} %bitcast.6, s32[2,9,2,32]{3,2,1,0:T(2,128)} %bitcast.5, s32[16]{0:T(128)} %send_hbm.1, s32[1,128]{1,0:T(1,128)} %bitcast.7, bf16[32,9,128,128]{3,2,1,0:T(8,128)(2,1)} %a_hbm.1, bf16[64,128,128]{2,1,0:T(8,128)(2,1)} %bitcast.4), custom_call_target="tpu_custom_call" | custom-call | tf_op jit(solution)/shard_map/sum_terms/pallas_call | solution.py:332
  35.7 1.3 %copy.8 = f32[32,128,128]{2,1,0:T(8,128)} copy(f32[32,128,128]{2,1,0:T(8,128)S(1)} %sum_terms.1) | data formatting | bytes 4194304

commit v5 on v4

--- a/solution.py
+++ b/solution.py
@@ -22,10 +22,10 @@
 ROW_STEP = 4
 ROW_RING = 16
 U = 4
-G = 154
-STEPS = 2
-STEP_ROWS = 5
-KEEP_ROWS = 2
+G = 308
+STEPS = 1
+STEP_ROWS = 10
+KEEP_ROWS = 4
 LEFTS = 2 * ENTRIES + 8
 OWN_BLOCKS = ROWS * SLOTS_P
 FAR_BLOCKS = 2 * HALO * SLOTS_P

time: 37.1 us -> 36.9 us (level)
  no operation moved by 1% of the time
where the time goes in v5:
time: 36.9 us; the launch traced here: 36.8 us
  Pallas kernels  35.5 us (96%)
  local copies, waits for them, and re-layouts  1.32 us (4%)
    pallas_call x1, Pallas kernels, sum_terms(): pl.pallas_call(terms_kernel, out_shape=pltpu.VMEM((OWN, B, B), F32), in_s...  35.5 us
    unnamed x1, local copies, waits for them, and re-layouts  1.32 us

profile of v5, /device:TPU:24, one launch (start us, length us, event | category | flops | bytes accessed | tf_op | source)
XLA Modules:
  0.0 36.8 jit_solution(11451735457450249414)
XLA Ops:
  0.0 35.5 %sum_terms.1 = f32[32,128,128]{2,1,0:T(8,128)S(1)} custom-call(s32[9,32]{1,0:T(8,128)} %bitcast.6, s32[2,9,2,32]{3,2,1,0:T(2,128)} %bitcast.5, s32[16]{0:T(128)} %send_hbm.1, s32[1,128]{1,0:T(1,128)} %bitcast.7, bf16[32,9,128,128]{3,2,1,0:T(8,128)(2,1)} %a_hbm.1, bf16[64,128,128]{2,1,0:T(8,128)(2,1)} %bitcast.4), custom_call_target="tpu_custom_call" | custom-call | tf_op jit(solution)/shard_map/sum_terms/pallas_call | solution.py:332
  35.5 1.3 %copy.8 = f32[32,128,128]{2,1,0:T(8,128)} copy(f32[32,128,128]{2,1,0:T(8,128)S(1)} %sum_terms.1) | data formatting | bytes 4194304
